TPU v7x, 128 devices: a whole 4x4x4 slice. The times are simulated.
128 devices in a mesh: oct: 4 (over y), box: 32 (over z, x, core).
Axes of the slice: x: 4, y: 4, z: 4, core: 2. Of those that a mesh axis runs over, the one named last changes fastest.
Arguments:
- coarse_multipole: bfloat16 [64, 8192], P(None, ('oct', 'box')), may hold values from -6 to 6
- fine_multipole: bfloat16 [64, 65536], P(None, ('oct', 'box')), may hold values from -6 to 6
- parent_local: float32 [64, 8192], P(None, ('oct', 'box')), may hold values from -4 to 4
- operators: bfloat16 [316, 64, 64], replicated, may hold values from -0.09375 to 0.09375
- child_maps: bfloat16 [8, 64, 64], replicated, may hold values from -0.75 to 0.75
- coarse_near_boxes: int32 [131072, 2], P(('oct', 'box')), may hold values from 0 to 63
- coarse_near_shift: int32 [131072], P(('oct', 'box')), may hold values from 0 to 315, as said below
- coarse_far_boxes: int32 [65536, 2], P(('oct', 'box')), may hold values from 0 to 63
- coarse_far_owner: int32 [65536, 1], P(('oct', 'box')), may hold values from 0 to 127, as said below
- coarse_far_shift: int32 [65536], P(('oct', 'box')), may hold values from 0 to 315, as said below
- fine_near_boxes: int32 [1048576, 2], P(('oct', 'box')), may hold values from 0 to 511
- fine_near_shift: int32 [1048576], P(('oct', 'box')), may hold values from 0 to 315, as said below
- fine_far_boxes: int32 [262144, 2], P(('oct', 'box')), may hold values from 0 to 511
- fine_far_owner: int32 [262144, 1], P(('oct', 'box')), may hold values from 0 to 127, as said below
- fine_far_shift: int32 [262144], P(('oct', 'box')), may hold values from 0 to 315, as said below
Outputs:
- coarse_local: bfloat16 [64, 8192], P(None, ('oct', 'box'))
- fine_local: bfloat16 [64, 65536], P(None, ('oct', 'box'))
Inputs may be any that keep to these rules, and one draw needn't show every extreme that they name: `coarse_far_owner`: for a listing device with index d, the owner (d + 1) mod 128 appears exactly 8 times among that device's rows, and every other owner fewer times. `fine_far_owner`: for a listing device with index d, the owner (d + 1) mod 128 appears exactly 32 times among that device's rows, and every other owner fewer times. `coarse_near_shift`: the rows of each aligned block of 128 rows share one translation vector. `coarse_far_shift`: the rows of each aligned block of 128 rows share one translation vector. `fine_near_shift`: the rows of each aligned block of 128 rows share one translation vector. `fine_far_shift`: the rows of each aligned block of 128 rows share one translation vector.
All inputs are finite; a program needn't handle non-finite values.
Results may differ from a plain program's by a relative error of at most 0.0033.
Values may be sent and summed in bfloat16 or wider, within the bound.
No kernel may reach another device: no remote copies, remote signals or barrier semaphores. Data moves between devices by JAX's collectives and lax.ppermute only.
A program may use at most 128 MiB of HBM per device.

v0:
```python
import jax
import jax.numpy as jnp
from jax import lax
from jax.experimental import pallas as pl
from jax.experimental.pallas import tpu as pltpu
from jax.sharding import PartitionSpec as P


F32 = jnp.float32
BF16 = jnp.bfloat16
I32 = jnp.int32

DEV = 128
RANK = 64
CAP_F = 32
CAP_C = 8
ROWS_F = CAP_F * RANK // 128
ROWS_C = CAP_C * RANK // 128
ROWS = 2 * (ROWS_F + ROWS_C)
HALF_CAP = CAP_F // 2
G_NEAR_F, G_FAR_F, G_NEAR_C, G_FAR_C = 64, 16, 8, 4
AT_FAR_F = G_NEAR_F
AT_NEAR_C = AT_FAR_F + G_FAR_F
AT_FAR_C = AT_NEAR_C + G_NEAR_C
GROUPS = 96
VMEM_LIMIT = 48 * 1024 * 1024


def mm(a, b):
    return lax.dot_general(a, b, (((1,), (0,)), ((), ())), preferred_element_type=F32)


def mm_nt(a, b):
    return lax.dot_general(a, b, (((1,), (1,)), ((), ())), preferred_element_type=F32)


def mm_tn(a, b):
    return lax.dot_general(a, b, (((0,), (0,)), ((), ())), preferred_element_type=F32)


def one_hot(row, count):
    n = row.shape[1]
    hit = lax.broadcasted_iota(I32, (count, n), 0) == row
    return jnp.where(hit, 1.0, 0.0).astype(BF16)


def half_stack(m):
    return jnp.concatenate([m[:, :256], m[:, 256:]], axis=0)


def pick_fine(stack, hot, row):
    both = mm(stack, hot)
    return jnp.where(row < 256, both[:RANK], both[RANK:])


def split_rows(values):
    high = values.astype(BF16)
    low = (values - high.astype(F32)).astype(BF16)
    return jnp.concatenate([high, low], axis=0)


def spread_fine(values, row):
    first = jnp.where(row < 256, values, 0.0)
    second = jnp.where(row < 256, 0.0, values)
    return split_rows(jnp.concatenate([first, second], axis=0))


def prefix_matrix():
    down = lax.broadcasted_iota(I32, (128, 256), 0)
    across = lax.broadcasted_iota(I32, (128, 256), 1)
    return jnp.where((down <= across) | (across >= 128), 1.0, 0.0).astype(BF16)


def route_kernel(f_owner, f_boxes, c_owner, c_boxes, slots_ref, f_pos, c_pos):
    prefix = prefix_matrix()

    def place(owner_ref, boxes_ref, pos_ref, blocks, cap, wide):
        carry = jnp.zeros((DEV, 128), F32)
        table = jnp.zeros((cap * (2 if wide else 1), DEV), F32)
        for b in range(blocks):
            lanes = slice(b * 128, (b + 1) * 128)
            hit = lax.broadcasted_iota(I32, (DEV, 128), 0) == owner_ref[:, lanes]
            hot = jnp.where(hit, 1.0, 0.0)
            counts = mm(hot.astype(BF16), prefix)
            seen = counts[:, :128] + carry
            pos = jnp.sum(jnp.where(hit, seen, 0.0), axis=0, keepdims=True) - 1.0
            carry = carry + counts[:, 128:]
            pos = pos.astype(I32)
            pos_ref[:, lanes] = pos
            slot = boxes_ref[1:2, lanes]
            here = lax.broadcasted_iota(I32, (cap, 128), 0) == pos
            low = jnp.where(here, (slot & 255).astype(F32), 0.0)
            if wide:
                high = jnp.where(here, (slot >> 8).astype(F32), 0.0)
                low = jnp.concatenate([low, high], axis=0)
            table = table + mm_nt(low.astype(BF16), hot.astype(BF16))
        if wide:
            table = table[:cap] + 256.0 * table[cap:]
        return table

    fine = place(f_owner, f_boxes, f_pos, 16, CAP_F, True)
    coarse = place(c_owner, c_boxes, c_pos, 4, CAP_C, False)
    rest = jnp.zeros((128 - CAP_F - CAP_C, DEV), F32)
    table = jnp.concatenate([fine, coarse, rest], axis=0)
    slots_ref[:, 0, :] = jnp.transpose(table).astype(I32)


def outgoing_kernel(
    ops, s_nf, s_ff, s_nc, s_fc, fm, cm, f_owner, f_boxes, f_pos, c_owner, c_boxes, c_pos,
    sel_ref, part_ref, kinds, kf, pm, hot_out, pm_c, flat,
):
    kinds[...] = jnp.zeros_like(kinds)
    kinds[0:AT_FAR_F] = s_nf[...]
    kinds[AT_FAR_F:AT_NEAR_C] = s_ff[...]
    kinds[AT_NEAR_C:AT_FAR_C] = s_nc[...]
    kinds[AT_FAR_C:AT_FAR_C + G_FAR_C] = s_fc[...]
    nt = ops.shape[2]
    hot_kind = jnp.where(
        kinds[:, 0:1] == lax.broadcasted_iota(I32, (GROUPS, nt), 1), 1.0, 0.0
    ).astype(BF16)
    for quad in range(RANK // 4):
        rows = ops[quad * 4:(quad + 1) * 4].reshape(256, nt)
        got = mm_nt(hot_kind, rows)
        for k in range(4):
            kf[pl.ds(quad * 4 + k, GROUPS, stride=RANK), :] = got[:, k * RANK:(k + 1) * RANK]
    sel_ref[...] = kf[...].reshape(GROUPS, RANK, RANK).astype(BF16)

    stack = half_stack(fm[...])
    for g in range(G_FAR_F):
        lanes = slice(g * 128, (g + 1) * 128)
        row = f_boxes[0:1, lanes]
        vec = pick_fine(stack, one_hot(row & 255, 256), row).astype(BF16)
        part = 2.0 * mm_tn(sel_ref[AT_FAR_F + g], vec)
        pos = f_pos[:, lanes]
        hot_out[:, lanes] = one_hot((pos >> 4) * DEV + f_owner[:, lanes], 2 * DEV)
        step = pos & (HALF_CAP - 1)
        for k in range(HALF_CAP):
            pm[k * RANK:(k + 1) * RANK, lanes] = jnp.where(step == k, part, 0.0).astype(BF16)
    for kp in range(HALF_CAP // 2):
        block = mm_nt(pm[kp * 128:(kp + 1) * 128, :], hot_out[...])
        for half in range(2):
            turned = jnp.transpose(block[:, half * DEV:(half + 1) * DEV])
            flat[pl.ds(half * (HALF_CAP // 2) + kp, DEV, stride=ROWS // 2), :] = turned

    hot_list = []
    for g in range(G_FAR_C):
        lanes = slice(g * 128, (g + 1) * 128)
        vec = mm(cm[...], one_hot(c_boxes[0:1, lanes], 64)).astype(BF16)
        part = mm_tn(sel_ref[AT_FAR_C + g], vec)
        pos = c_pos[:, lanes]
        hot_list.append(one_hot(c_owner[:, lanes], DEV))
        for k in range(CAP_C):
            pm_c[k * RANK:(k + 1) * RANK, lanes] = jnp.where(pos == k, part, 0.0).astype(BF16)
    hot_c = jnp.concatenate(hot_list, axis=1)
    for kp in range(CAP_C // 2):
        block = mm_nt(pm_c[kp * 128:(kp + 1) * 128, :], hot_c)
        flat[pl.ds(ROWS_F + kp, DEV, stride=ROWS // 2), :] = jnp.transpose(block)
    part_ref[...] = flat[...].reshape(DEV, ROWS // 2, 128).astype(BF16)


def reply_kernel(slots, fm, cm, part, out_ref, flat):
    table = jnp.transpose(slots[:, 0, :].astype(F32)).astype(I32)
    stack = half_stack(fm[...])
    for kp in range(ROWS_F):
        row = jnp.concatenate([table[2 * kp:2 * kp + 1], table[2 * kp + 1:2 * kp + 2]], axis=1)
        vec = pick_fine(stack, one_hot(row & 255, 256), row)
        both = jnp.concatenate([vec[:, :DEV], vec[:, DEV:]], axis=0)
        flat[pl.ds(kp, DEV, stride=ROWS // 2), :] = jnp.transpose(both)
    for kp in range(ROWS_C):
        at = CAP_F + 2 * kp
        row = jnp.concatenate([table[at:at + 1], table[at + 1:at + 2]], axis=1)
        vec = mm(cm[...], one_hot(row, 64))
        both = jnp.concatenate([vec[:, :DEV], vec[:, DEV:]], axis=0)
        flat[pl.ds(ROWS_F + kp, DEV, stride=ROWS // 2), :] = jnp.transpose(both)
    replies = flat[...].reshape(DEV, ROWS // 2, 128)
    out_ref[...] = jnp.concatenate([replies, part[...].astype(F32)], axis=1).astype(BF16)


def near_kernel(sel, fm, cm, f_boxes, c_boxes, f_out, c_out):
    stack = half_stack(fm[...])
    f_out[...] = jnp.zeros_like(f_out)

    def step(i, carry):
        lanes = pl.ds(pl.multiple_of(i * 256, 256), 256)
        first = f_boxes[0:1, lanes]
        second = f_boxes[1:2, lanes]
        hot_1 = one_hot(first & 255, 256)
        hot_2 = one_hot(second & 255, 256)
        vec_1 = pick_fine(stack, hot_1, first).astype(BF16)
        vec_2 = pick_fine(stack, hot_2, second).astype(BF16)
        to_1, to_2 = [], []
        for k in range(2):
            op = sel[2 * i + k]
            cut = slice(k * 128, (k + 1) * 128)
            to_1.append(mm(op, vec_2[:, cut]))
            to_2.append(mm_tn(op, vec_1[:, cut]))
        to_1 = jnp.concatenate(to_1, axis=1)
        to_2 = jnp.concatenate(to_2, axis=1)
        f_out[...] += mm_nt(spread_fine(to_1, first), hot_1) + mm_nt(
            spread_fine(to_2, second), hot_2
        )
        return carry

    lax.fori_loop(0, G_NEAR_F // 2, step, 0)
    total = jnp.zeros((2 * RANK, 64), F32)
    for g in range(G_NEAR_C):
        lanes = slice(g * 128, (g + 1) * 128)
        hot_1 = one_hot(c_boxes[0:1, lanes], 64)
        hot_2 = one_hot(c_boxes[1:2, lanes], 64)
        vec_1 = mm(cm[...], hot_1).astype(BF16)
        vec_2 = mm(cm[...], hot_2).astype(BF16)
        op = sel[AT_NEAR_C + g]
        total = total + mm_nt(split_rows(mm(op, vec_2)), hot_1)
        total = total + mm_nt(split_rows(mm_tn(op, vec_1)), hot_2)
    c_out[...] = total


def final_kernel(
    got, slots, sel, f_near, c_near, parent, maps, f_owner, f_boxes, f_pos, c_owner, c_boxes, c_pos,
    c_ref, f_ref, flat, held, turned_c,
):
    flat[...] = got[...].astype(F32).reshape(DEV * ROWS, 128)
    table = jnp.transpose(slots[:, 0, :].astype(F32)).astype(I32)

    def turned(row):
        return jnp.transpose(flat[pl.ds(row, DEV, stride=ROWS), :])

    for kp in range(ROWS_C):
        turned_c[kp * 128:(kp + 1) * 128, :] = turned(ROWS_F + kp).astype(BF16)
    total_c = c_near[...]
    for g in range(G_FAR_C):
        lanes = slice(g * 128, (g + 1) * 128)
        found = mm(turned_c[...], one_hot(c_owner[:, lanes], DEV))
        pos = c_pos[:, lanes]
        vec = jnp.zeros((RANK, 128), F32)
        for k in range(CAP_C):
            vec = jnp.where(pos == k, found[k * RANK:(k + 1) * RANK], vec)
        to_1 = mm(sel[AT_FAR_C + g], vec.astype(BF16))
        total_c = total_c + mm_nt(split_rows(to_1), one_hot(c_boxes[0:1, lanes], 64))
    for kp in range(ROWS_C):
        arrived = turned(ROWS // 2 + ROWS_F + kp).astype(BF16)
        for par in range(2):
            at = CAP_F + 2 * kp + par
            add = mm_nt(arrived[par * RANK:(par + 1) * RANK], one_hot(table[at:at + 1], 64))
            total_c = total_c + jnp.concatenate([add, jnp.zeros_like(add)], axis=0)
    coarse = (parent[...] + total_c[:RANK] + total_c[RANK:]).astype(BF16)
    c_ref[...] = coarse

    box = lax.broadcasted_iota(I32, (64, 512), 1)
    parent_of = jnp.where((box >> 3) == lax.broadcasted_iota(I32, (64, 512), 0), 1.0, 0.0)
    wide = mm(coarse, parent_of.astype(BF16)).astype(BF16)
    start = jnp.zeros((RANK, 512), F32)
    for k in range(8):
        start = jnp.where((box & 7) == k, mm(maps[k], wide), start)

    for half in range(2):
        for kp in range(HALF_CAP // 2):
            held[kp * 128:(kp + 1) * 128, half * DEV:(half + 1) * DEV] = turned(
                half * (HALF_CAP // 2) + kp
            ).astype(BF16)
    total = f_near[...]
    for i in range(G_FAR_F // 2):
        lanes = slice(i * 256, (i + 1) * 256)
        pos = f_pos[:, lanes]
        found = mm(held[...], one_hot((pos >> 4) * DEV + f_owner[:, lanes], 2 * DEV))
        where = pos & (HALF_CAP - 1)
        vec = jnp.zeros((RANK, 256), F32)
        for k in range(HALF_CAP):
            vec = jnp.where(where == k, found[k * RANK:(k + 1) * RANK], vec)
        vec = vec.astype(BF16)
        to_1 = jnp.concatenate(
            [mm(sel[AT_FAR_F + 2 * i + k], vec[:, k * 128:(k + 1) * 128]) for k in range(2)], axis=1
        )
        first = f_boxes[0:1, lanes]
        total = total + mm_nt(spread_fine(to_1, first), one_hot(first & 255, 256))
    added = jnp.zeros((2 * RANK, 256), F32)
    for kp in range(ROWS_F):
        arrived = turned(ROWS // 2 + kp)
        row = jnp.concatenate([table[2 * kp:2 * kp + 1], table[2 * kp + 1:2 * kp + 2]], axis=1)
        side = jnp.concatenate([arrived[:RANK], arrived[RANK:]], axis=1)
        both = jnp.concatenate(
            [jnp.where(row < 256, side, 0.0), jnp.where(row < 256, 0.0, side)], axis=0
        )
        added = added + mm_nt(both.astype(BF16), one_hot(row & 255, 256))
    total = 2.0 * (total[:2 * RANK] + total[2 * RANK:]) + added
    fine = start + jnp.concatenate([total[:RANK], total[RANK:]], axis=1)
    f_ref[...] = fine.astype(BF16)


def call(kernel, out_shape, scratch, flops, nbytes, *args):
    return pl.pallas_call(
        kernel,
        out_shape=out_shape,
        scratch_shapes=scratch,
        compiler_params=pltpu.CompilerParams(vmem_limit_bytes=VMEM_LIMIT),
        cost_estimate=pl.CostEstimate(flops=flops, bytes_accessed=nbytes, transcendentals=0),
    )(*args)


def on_device(
    coarse_multipole,
    fine_multipole,
    parent_local,
    operators,
    child_maps,
    coarse_near_boxes,
    coarse_near_shift,
    coarse_far_boxes,
    coarse_far_owner,
    coarse_far_shift,
    fine_near_boxes,
    fine_near_shift,
    fine_far_boxes,
    fine_far_owner,
    fine_far_shift,
):
    def sds(shape, dtype):
        return jax.ShapeDtypeStruct(shape, dtype)

    fm, cm = fine_multipole, coarse_multipole
    f_owner, c_owner = fine_far_owner.T, coarse_far_owner.T
    f_far, c_far = fine_far_boxes.T, coarse_far_boxes.T
    ops = jnp.transpose(operators, (1, 2, 0))

    slots, f_pos, c_pos = call(
        route_kernel,
        (sds((DEV, 1, 128), I32), sds((1, 2048), I32), sds((1, 512), I32)),
        [],
        10**9,
        10**6,
        f_owner, f_far, c_owner, c_far,
    )
    asked = lax.all_to_all(slots, ("oct", "box"), split_axis=0, concat_axis=0, tiled=True)
    sel, part = call(
        outgoing_kernel,
        (sds((GROUPS, RANK, RANK), BF16), sds((DEV, ROWS // 2, 128), BF16)),
        [
            pltpu.VMEM((GROUPS, 128), I32),
            pltpu.VMEM((GROUPS * RANK, RANK), F32),
            pltpu.VMEM((HALF_CAP * RANK, 2048), BF16),
            pltpu.VMEM((2 * DEV, 2048), BF16),
            pltpu.VMEM((CAP_C * RANK, 512), BF16),
            pltpu.VMEM((DEV * ROWS // 2, 128), F32),
        ],
        5 * 10**9,
        10**7,
        ops,
        fine_near_shift.reshape(-1, 128),
        fine_far_shift.reshape(-1, 128),
        coarse_near_shift.reshape(-1, 128),
        coarse_far_shift.reshape(-1, 128),
        fm, cm, f_owner, f_far, f_pos, c_owner, c_far, c_pos,
    )
    sent = call(
        reply_kernel,
        sds((DEV, ROWS, 128), BF16),
        [pltpu.VMEM((DEV * ROWS // 2, 128), F32)],
        10**9,
        10**6,
        asked, fm, cm, part,
    )
    got = lax.all_to_all(sent, ("oct", "box"), split_axis=0, concat_axis=0, tiled=True)
    f_near, c_near = call(
        near_kernel,
        (sds((4 * RANK, 256), F32), sds((2 * RANK, 64), F32)),
        [],
        10**10,
        10**7,
        sel, fm, cm, fine_near_boxes.T, coarse_near_boxes.T,
    )
    return call(
        final_kernel,
        (sds((RANK, 64), BF16), sds((RANK, 512), BF16)),
        [
            pltpu.VMEM((DEV * ROWS, 128), F32),
            pltpu.VMEM((HALF_CAP * RANK, 2 * DEV), BF16),
            pltpu.VMEM((CAP_C * RANK, DEV), BF16),
        ],
        3 * 10**9,
        10**7,
        got, asked, sel, f_near, c_near, parent_local, child_maps,
        f_owner, f_far, f_pos, c_owner, c_far, c_pos,
    )


def solution(mesh):
    both = ("oct", "box")
    return jax.shard_map(
        on_device,
        mesh=mesh,
        in_specs=(
            P(None, both),
            P(None, both),
            P(None, both),
            P(),
            P(),
            P(both, None),
            P(both),
            P(both, None),
            P(both, None),
            P(both),
            P(both, None),
            P(both),
            P(both, None),
            P(both, None),
            P(both),
        ),
        out_specs=(P(None, both), P(None, both)),
        check_vma=False,
    )
```

profile of v0, /device:TPU:1, one launch (start us, length us, event | category | flops | bytes accessed | tf_op | source)
XLA Modules:
  0.0 70.4 jit_solution(11615153390758361153)
XLA Ops:
  0.6 0.0 copy-start.7
  0.6 0.7 %copy-done.7 = s32[2048,2]{0,1:T(2,128)S(1)} copy-done((s32[2048,2]{0,1:T(2,128)S(1)}, s32[2048,2]{0,1:T(2,128)}, u32[]{:S(2)}) %copy-start.7) | copy-done | bytes 16408
  1.4 0.0 copy-start.11
  1.4 0.7 copy-done.11
  2.0 0.0 copy-start.14
  2.1 0.7 copy-done.14
  2.7 0.0 copy-start.17
  2.7 0.7 copy-done.17
  3.4 0.0 copy-start.2
  3.4 0.0 copy-start.4
  3.4 0.0 copy-start.6
  3.4 0.0 copy-start.8
  3.4 0.0 copy-start.9
  3.4 0.0 copy-start.12
  3.5 0.0 copy-start.13
  3.5 0.0 copy-start.15
  3.5 0.0 copy-start.16
  3.5 0.0 copy-start.18
  3.5 1.7 %shard_map.158 = (s32[128,1,128]{2,1,0:T(1,128)}, s32[1,2048]{1,0:T(1,128)S(1)}, s32[1,512]{1,0:T(1,128)S(1)}) custom-call(s32[1,2048]{1,0:T(1,128)S(1)} %bitcast.19, s32[2,2048]{1,0:T(2,128)S(1)} %bitcast.14, s32[1,512]{1,0:T(1,128)S(1)} %bitcast.27, s32[2,512]{1,0:T(2,128)S(1)} %bitcast.23), custom_call_target="tpu_custom_call" | custom-call | flops 1000000000 | bytes 1000000 | tf_op jit(solution)/shard_map/pallas_call | solution.py:291
  5.1 11.5 %all-to-all-start = ((s32[128,1,128]{2,1,0:T(1,128)}), s32[128,1,128]{2,1,0:T(1,128)S(1)}, u32[]{:S(2)}, u32[]{:S(2)}) async-start(s32[128,1,128]{2,1,0:T(1,128)} %get-tuple-element.9), calls=%async_computation | async-start | bytes 131072 | tf_op jit(solution)/shard_map/all_to_all | solution.py:333
  16.7 0.0 copy-done.2
  16.7 0.0 copy-done.4
  16.7 0.0 copy-done.6
  16.7 0.0 copy-done.8
  16.7 0.0 copy-done.9
  16.7 0.0 copy-done.12
  16.7 0.0 copy-done.13
  16.7 0.0 copy-done.15
  16.7 0.0 copy-done.16
  16.7 0.0 copy-done.18
  16.8 0.0 copy-start
  16.8 1.9 %copy-done = bf16[316,64,64]{0,2,1:T(8,128)(2,1)S(1)} copy-done((bf16[316,64,64]{0,2,1:T(8,128)(2,1)S(1)}, bf16[316,64,64]{0,2,1:T(8,128)(2,1)}, u32[]{:S(2)}) %copy-start) | copy-done | bytes 2588696
  18.6 9.4 %shard_map.159 = (bf16[96,64,64]{2,1,0:T(8,128)(2,1)S(1)}, bf16[128,20,128]{2,1,0:T(8,128)(2,1)S(1)}) custom-call(bf16[64,64,316]{2,1,0:T(8,128)(2,1)S(1)} %bitcast.11, s32[64,128]{1,0:T(8,128)S(1)} %bitcast.13, s32[16,128]{1,0:T(8,128)S(1)} %bitcast.17, s32[8,128]{1,0:T(8,128)S(1)} %bitcast.22, s32[4,128]{1,0:T(4,128)S(1)} %bitcast.26, ...), custom_call_target="tpu_custom_call" | custom-call | flops 5000000000 | bytes 10000000 | tf_op jit(solution)/shard_map/pallas_call | solution.py:291
  28.0 0.0 all-to-all-done.slots
  28.0 2.0 %shard_map.160 = bf16[128,40,128]{2,1,0:T(8,128)(2,1)} custom-call(s32[128,1,128]{2,1,0:T(1,128)S(1)} %all-to-all-done.slots, bf16[64,512]{1,0:T(8,128)(2,1)S(1)} %copy-done.2, bf16[64,64]{1,0:T(8,128)(2,1)S(1)} %copy-done.6, bf16[128,20,128]{2,1,0:T(8,128)(2,1)S(1)} %get-tuple-element.12.part), custom_call_target="tpu_custom_call" | custom-call | flops 1000000000 | bytes 1000000 | tf_op jit(solution)/shard_map/pallas_call | solution.py:291
  30.0 0.0 copy-start.3
  30.0 0.0 copy-start.10
  30.0 9.8 %all-to-all-start.1 = ((bf16[128,40,128]{2,1,0:T(8,128)(2,1)}), bf16[128,40,128]{2,1,0:T(8,128)(2,1)S(1)}, u32[]{:S(2)}, u32[]{:S(2)}) async-start(bf16[128,40,128]{2,1,0:T(8,128)(2,1)} %shard_map.160), calls=%async_computation.1 | async-start | bytes 2621440 | tf_op jit(solution)/shard_map/all_to_all | solution.py:362
  39.8 0.0 copy-done.3
  39.8 0.0 copy-done.10
  39.8 0.0 copy-start.1
  39.8 0.0 copy-start.5
  39.8 19.4 %shard_map.161 = (f32[256,256]{1,0:T(8,128)S(1)}, f32[128,64]{1,0:T(8,128)S(1)}) custom-call(bf16[96,64,64]{2,1,0:T(8,128)(2,1)S(1)} %get-tuple-element.13.sel, bf16[64,512]{1,0:T(8,128)(2,1)S(1)} %copy-done.2, bf16[64,64]{1,0:T(8,128)(2,1)S(1)} %copy-done.6, s32[2,8192]{1,0:T(2,128)S(1)} %bitcast.12, s32[2,1024]{1,0:T(2,128)S(1)} %bitcast.18), custom_call_target="tpu_custom_call" | custom-call | flops 10000000000 | bytes 10000000 | tf_op jit(solution)/shard_map/pallas_call | solution.py:291
  59.2 0.0 copy-start.19
  59.2 0.7 copy-done.19
  59.9 2.0 %all-to-all-done.1.got = bf16[128,40,128]{2,1,0:T(8,128)(2,1)S(1)} async-done(((bf16[128,40,128]{2,1,0:T(8,128)(2,1)}), bf16[128,40,128]{2,1,0:T(8,128)(2,1)S(1)}, u32[]{:S(2)}, u32[]{:S(2)}) %all-to-all-start.1) | async-done | bytes 1310752 | tf_op jit(solution)/shard_map/all_to_all | solution.py:362
  61.9 0.0 copy-done.1
  61.9 0.0 copy-done.5
  61.9 0.0 copy-start.20
  61.9 0.9 %copy-done.20 = f32[256,256]{1,0:T(8,128)S(1)} copy-done((f32[256,256]{1,0:T(8,128)S(1)}, f32[256,256]{1,0:T(8,128)}, u32[]{:S(2)}) %copy-start.20) | copy-done | bytes 262168
  62.9 7.5 %shard_map.162 = (bf16[64,64]{1,0:T(8,128)(2,1)}, bf16[64,512]{1,0:T(8,128)(2,1)}) custom-call(bf16[128,40,128]{2,1,0:T(8,128)(2,1)S(1)} %all-to-all-done.1.got, s32[128,1,128]{2,1,0:T(1,128)S(1)} %all-to-all-done.slots, bf16[96,64,64]{2,1,0:T(8,128)(2,1)S(1)} %get-tuple-element.13.sel, f32[256,256]{1,0:T(8,128)S(1)} %copy-done.20, ...), custom_call_target="tpu_custom_call" | custom-call | flops 3000000000 | bytes 10000000 | tf_op jit(solution)/shard_map/pallas_call | solution.py:291
Async XLA Ops:
  0.6 0.7 %copy-start.7 = (s32[2048,2]{0,1:T(2,128)S(1)}, s32[2048,2]{0,1:T(2,128)}, u32[]{:S(2)}) copy-start(s32[2048,2]{0,1:T(2,128)} %param.27) | copy-start | bytes 49156
  1.4 0.7 copy-start.11
  2.0 0.7 copy-start.14
  2.7 0.7 copy-start.17
  3.4 13.2 %copy-start.2 = (bf16[64,512]{1,0:T(8,128)(2,1)S(1)}, bf16[64,512]{1,0:T(8,128)(2,1)}, u32[]{:S(2)}) copy-start(bf16[64,512]{1,0:T(8,128)(2,1)} %fm.5) | copy-start | bytes 196612
  3.4 13.2 %copy-start.4 = (s32[8192]{0:T(1024)S(1)}, s32[8192]{0:T(1024)}, u32[]{:S(2)}) copy-start(s32[8192]{0:T(1024)} %param.26) | copy-start | bytes 98308
  3.4 13.3 %copy-start.6 = (bf16[64,64]{1,0:T(8,128)(2,1)S(1)}, bf16[64,64]{1,0:T(8,128)(2,1)}, u32[]{:S(2)}) copy-start(bf16[64,64]{1,0:T(8,128)(2,1)} %cm.5) | copy-start | bytes 24580
  3.4 13.3 %copy-start.8 = (s32[2048,2]{0,1:T(2,128)S(1)}, s32[2048,2]{0,1:T(2,128)}, u32[]{:S(2)}) copy-start(s32[2048,2]{0,1:T(2,128)} %param.27) | copy-start | bytes 49156
  3.4 13.3 %copy-start.9 = (s32[2048]{0:T(1024)S(1)}, s32[2048]{0:T(1024)}, u32[]{:S(2)}) copy-start(s32[2048]{0:T(1024)} %param.29) | copy-start | bytes 24580
  3.4 13.3 %copy-start.12 = (s32[2048,1]{0,1:T(1,128)S(1)}, s32[2048,1]{0,1:T(1,128)}, u32[]{:S(2)}) copy-start(s32[2048,1]{0,1:T(1,128)} %param.28) | copy-start | bytes 24580
  3.5 13.3 %copy-start.13 = (s32[1024]{0:T(1024)S(1)}, s32[1024]{0:T(1024)}, u32[]{:S(2)}) copy-start(s32[1024]{0:T(1024)} %param.21) | copy-start | bytes 12292
  3.5 13.3 %copy-start.15 = (s32[512,2]{0,1:T(2,128)S(1)}, s32[512,2]{0,1:T(2,128)}, u32[]{:S(2)}) copy-start(s32[512,2]{0,1:T(2,128)} %param.22) | copy-start | bytes 12292
  3.5 13.3 %copy-start.16 = (s32[512]{0:T(512)S(1)}, s32[512]{0:T(512)}, u32[]{:S(2)}) copy-start(s32[512]{0:T(512)} %param.24) | copy-start | bytes 6148
  3.5 13.3 %copy-start.18 = (s32[512,1]{0,1:T(1,128)S(1)}, s32[512,1]{0,1:T(1,128)}, u32[]{:S(2)}) copy-start(s32[512,1]{0,1:T(1,128)} %param.23) | copy-start | bytes 6148
  5.1 22.9 %all-to-all-start = ((s32[128,1,128]{2,1,0:T(1,128)}), s32[128,1,128]{2,1,0:T(1,128)S(1)}, u32[]{:S(2)}, u32[]{:S(2)}) async-start(s32[128,1,128]{2,1,0:T(1,128)} %get-tuple-element.9), calls=%async_computation | async-start | bytes 131072 | tf_op jit(solution)/shard_map/all_to_all | solution.py:333
  16.8 1.9 %copy-start = (bf16[316,64,64]{0,2,1:T(8,128)(2,1)S(1)}, bf16[316,64,64]{0,2,1:T(8,128)(2,1)}, u32[]{:S(2)}) copy-start(bf16[316,64,64]{0,2,1:T(8,128)(2,1)} %param.18) | copy-start | bytes 7766020
  30.0 9.8 %copy-start.3 = (s32[8192,2]{0,1:T(2,128)S(1)}, s32[8192,2]{0,1:T(2,128)}, u32[]{:S(2)}) copy-start(s32[8192,2]{0,1:T(2,128)} %param.25) | copy-start | bytes 196612
  30.0 9.8 %copy-start.10 = (s32[1024,2]{0,1:T(2,128)S(1)}, s32[1024,2]{0,1:T(2,128)}, u32[]{:S(2)}) copy-start(s32[1024,2]{0,1:T(2,128)} %param.20) | copy-start | bytes 24580
  30.0 31.9 %all-to-all-start.1 = ((bf16[128,40,128]{2,1,0:T(8,128)(2,1)}), bf16[128,40,128]{2,1,0:T(8,128)(2,1)S(1)}, u32[]{:S(2)}, u32[]{:S(2)}) async-start(bf16[128,40,128]{2,1,0:T(8,128)(2,1)} %shard_map.160), calls=%async_computation.1 | async-start | bytes 2621440 | tf_op jit(solution)/shard_map/all_to_all | solution.py:362
  39.8 22.1 %copy-start.1 = (bf16[8,64,64]{2,1,0:T(8,128)(2,1)S(1)}, bf16[8,64,64]{2,1,0:T(8,128)(2,1)}, u32[]{:S(2)}) copy-start(bf16[8,64,64]{2,1,0:T(8,128)(2,1)} %maps.1) | copy-start | bytes 196612
  39.8 22.1 %copy-start.5 = (f32[64,64]{1,0:T(8,128)S(1)}, f32[64,64]{1,0:T(8,128)}, u32[]{:S(2)}) copy-start(f32[64,64]{1,0:T(8,128)} %parent.1) | copy-start | bytes 49156
  59.2 0.7 copy-start.19
  61.9 1.0 %copy-start.20 = (f32[256,256]{1,0:T(8,128)S(1)}, f32[256,256]{1,0:T(8,128)}, u32[]{:S(2)}) copy-start(f32[256,256]{1,0:T(8,128)} %copy-done.19) | copy-start | bytes 786436
where the time goes:
time: 70.8 us; the launch traced here: 70.4 us
  Pallas kernels  39.9 us (56%)
  starting transfers between devices  21.3 us (30%)
  local copies, waits for them, and re-layouts  6.36 us (9%)
  waiting for transfers between devices  2.02 us (3%)
  between operations  0.87 us (1%)
    pallas_call x5, Pallas kernels, call(): pl.pallas_call(kernel, out_shape=out_shape, scratch_shapes=scratch, compi...  39.9 us
    all_to_all x1, starting transfers between devices, on_device(): lax.all_to_all(slots, ('oct', 'box'), split_axis=0, concat_axis=0, tiled=...  11.5 us
    all_to_all x1, starting transfers between devices, on_device(): lax.all_to_all(sent, ('oct', 'box'), split_axis=0, concat_axis=0, tiled=T...  9.77 us
    unnamed x42, local copies, waits for them, and re-layouts  6.36 us
    all_to_all x1, waiting for transfers between devices, on_device(): lax.all_to_all(sent, ('oct', 'box'), split_axis=0, concat_axis=0, tiled=T...  2.02 us
  transfers between devices with their start and end apart: 2, of which 1 were waited for; matrix products, arithmetic and copies ran while one was open for 0% of the time, Pallas kernels for 41%

commit v1 on v0

--- a/solution.py
+++ b/solution.py
@@ -23,6 +23,9 @@
 AT_NEAR_C = AT_FAR_F + G_FAR_F
 AT_FAR_C = AT_NEAR_C + G_NEAR_C
 GROUPS = 96
+NEAR_BLOCK = 4096
+FAR_BLOCK = 2048
+PM_ROWS = 512
 VMEM_LIMIT = 48 * 1024 * 1024
 
 
@@ -40,8 +43,9 @@
 
 def one_hot(row, count):
     n = row.shape[1]
-    hit = lax.broadcasted_iota(I32, (count, n), 0) == row
-    return jnp.where(hit, 1.0, 0.0).astype(BF16)
+    at = lax.broadcasted_iota(I32, (count, n), 0).astype(BF16)
+    hit = at == jnp.broadcast_to(row.astype(BF16), (count, n))
+    return jnp.where(hit, jnp.ones((), BF16), jnp.zeros((), BF16))
 
 
 def half_stack(m):
@@ -126,21 +130,29 @@
     sel_ref[...] = kf[...].reshape(GROUPS, RANK, RANK).astype(BF16)
 
     stack = half_stack(fm[...])
-    for g in range(G_FAR_F):
-        lanes = slice(g * 128, (g + 1) * 128)
-        row = f_boxes[0:1, lanes]
-        vec = pick_fine(stack, one_hot(row & 255, 256), row).astype(BF16)
-        part = 2.0 * mm_tn(sel_ref[AT_FAR_F + g], vec)
-        pos = f_pos[:, lanes]
-        hot_out[:, lanes] = one_hot((pos >> 4) * DEV + f_owner[:, lanes], 2 * DEV)
-        step = pos & (HALF_CAP - 1)
-        for k in range(HALF_CAP):
-            pm[k * RANK:(k + 1) * RANK, lanes] = jnp.where(step == k, part, 0.0).astype(BF16)
-    for kp in range(HALF_CAP // 2):
-        block = mm_nt(pm[kp * 128:(kp + 1) * 128, :], hot_out[...])
-        for half in range(2):
-            turned = jnp.transpose(block[:, half * DEV:(half + 1) * DEV])
-            flat[pl.ds(half * (HALF_CAP // 2) + kp, DEV, stride=ROWS // 2), :] = turned
+    row = f_boxes[0:1, :]
+    vec = pick_fine(stack, one_hot(row & 255, 256), row).astype(BF16)
+    part = jnp.concatenate(
+        [
+            mm_tn(sel_ref[AT_FAR_F + g], vec[:, g * 128:(g + 1) * 128])
+            for g in range(G_FAR_F)
+        ],
+        axis=1,
+    )
+    part = (2.0 * part).astype(BF16)
+    pos = f_pos[...]
+    hot_out[...] = one_hot((pos >> 4) * DEV + f_owner[...], 2 * DEV)
+    step = jnp.broadcast_to((pos & (HALF_CAP - 1)).astype(BF16), part.shape)
+    none = jnp.zeros((), BF16)
+    for k in range(HALF_CAP):
+        pm[k * RANK:(k + 1) * RANK, :] = jnp.where(step == jnp.asarray(k, BF16), part, none)
+    for j in range(HALF_CAP * RANK // PM_ROWS):
+        big = mm_nt(pm[j * PM_ROWS:(j + 1) * PM_ROWS, :], hot_out[...])
+        for i in range(PM_ROWS // 128):
+            kp = j * (PM_ROWS // 128) + i
+            for half in range(2):
+                turned = jnp.transpose(big[i * 128:(i + 1) * 128, half * DEV:(half + 1) * DEV])
+                flat[pl.ds(half * (HALF_CAP // 2) + kp, DEV, stride=ROWS // 2), :] = turned
 
     hot_list = []
     for g in range(G_FAR_C):
@@ -181,7 +193,7 @@
     f_out[...] = jnp.zeros_like(f_out)
 
     def step(i, carry):
-        lanes = pl.ds(pl.multiple_of(i * 256, 256), 256)
+        lanes = pl.ds(pl.multiple_of(i * NEAR_BLOCK, NEAR_BLOCK), NEAR_BLOCK)
         first = f_boxes[0:1, lanes]
         second = f_boxes[1:2, lanes]
         hot_1 = one_hot(first & 255, 256)
@@ -189,19 +201,19 @@
         vec_1 = pick_fine(stack, hot_1, first).astype(BF16)
         vec_2 = pick_fine(stack, hot_2, second).astype(BF16)
         to_1, to_2 = [], []
-        for k in range(2):
-            op = sel[2 * i + k]
+        for k in range(NEAR_BLOCK // 128):
+            op = sel[NEAR_BLOCK // 128 * i + k]
             cut = slice(k * 128, (k + 1) * 128)
             to_1.append(mm(op, vec_2[:, cut]))
             to_2.append(mm_tn(op, vec_1[:, cut]))
         to_1 = jnp.concatenate(to_1, axis=1)
         to_2 = jnp.concatenate(to_2, axis=1)
-        f_out[...] += mm_nt(spread_fine(to_1, first), hot_1) + mm_nt(
-            spread_fine(to_2, second), hot_2
-        )
+        both = jnp.concatenate([spread_fine(to_1, first), spread_fine(to_2, second)], axis=1)
+        hots = jnp.concatenate([hot_1, hot_2], axis=1)
+        f_out[...] += mm_nt(both, hots)
         return carry
 
-    lax.fori_loop(0, G_NEAR_F // 2, step, 0)
+    lax.fori_loop(0, G_NEAR_F * 128 // NEAR_BLOCK, step, 0)
     total = jnp.zeros((2 * RANK, 64), F32)
     for g in range(G_NEAR_C):
         lanes = slice(g * 128, (g + 1) * 128)
@@ -259,29 +271,34 @@
                 half * (HALF_CAP // 2) + kp
             ).astype(BF16)
     total = f_near[...]
-    for i in range(G_FAR_F // 2):
-        lanes = slice(i * 256, (i + 1) * 256)
+    for i in range(2048 // FAR_BLOCK):
+        lanes = slice(i * FAR_BLOCK, (i + 1) * FAR_BLOCK)
         pos = f_pos[:, lanes]
         found = mm(held[...], one_hot((pos >> 4) * DEV + f_owner[:, lanes], 2 * DEV))
         where = pos & (HALF_CAP - 1)
-        vec = jnp.zeros((RANK, 256), F32)
+        vec = jnp.zeros((RANK, FAR_BLOCK), F32)
         for k in range(HALF_CAP):
             vec = jnp.where(where == k, found[k * RANK:(k + 1) * RANK], vec)
         vec = vec.astype(BF16)
+        each = FAR_BLOCK // 128
         to_1 = jnp.concatenate(
-            [mm(sel[AT_FAR_F + 2 * i + k], vec[:, k * 128:(k + 1) * 128]) for k in range(2)], axis=1
+            [mm(sel[AT_FAR_F + each * i + k], vec[:, k * 128:(k + 1) * 128]) for k in range(each)],
+            axis=1,
         )
         first = f_boxes[0:1, lanes]
         total = total + mm_nt(spread_fine(to_1, first), one_hot(first & 255, 256))
-    added = jnp.zeros((2 * RANK, 256), F32)
+    sides, hots = [], []
     for kp in range(ROWS_F):
         arrived = turned(ROWS // 2 + kp)
         row = jnp.concatenate([table[2 * kp:2 * kp + 1], table[2 * kp + 1:2 * kp + 2]], axis=1)
         side = jnp.concatenate([arrived[:RANK], arrived[RANK:]], axis=1)
-        both = jnp.concatenate(
-            [jnp.where(row < 256, side, 0.0), jnp.where(row < 256, 0.0, side)], axis=0
+        none = jnp.zeros((), BF16)
+        upper = jnp.broadcast_to(row, side.shape) < 256
+        sides.append(
+            jnp.concatenate([jnp.where(upper, side, 0.0), jnp.where(upper, 0.0, side)], axis=0).astype(BF16)
         )
-        added = added + mm_nt(both.astype(BF16), one_hot(row & 255, 256))
+        hots.append(one_hot(row & 255, 256))
+    added = mm_nt(jnp.concatenate(sides, axis=1), jnp.concatenate(hots, axis=1))
     total = 2.0 * (total[:2 * RANK] + total[2 * RANK:]) + added
     fine = start + jnp.concatenate([total[:RANK], total[RANK:]], axis=1)
     f_ref[...] = fine.astype(BF16)

time: 70.8 us -> 64.7 us (0.914)
  Pallas kernels: 39.9 us -> 20.9 us
  waiting for transfers between devices: 2.02 us -> 16.9 us
  starting transfers between devices: 21.3 us -> 19.3 us
    pallas_call x5, Pallas kernels: 39.9 us -> 20.9 us  [call(): pl.pallas_call(kernel, out_shape=out_shape, scratch_shapes=scratch, compi...]
    all_to_all x1, waiting for transfers between devices: 2.02 us -> 14.9 us  [on_device(): lax.all_to_all(sent, ('oct', 'box'), split_axis=0, concat_axis=0, tiled=T...]
    all_to_all x1, starting transfers between devices: 9.77 us -> 7.79 us  [on_device(): lax.all_to_all(sent, ('oct', 'box'), split_axis=0, concat_axis=0, tiled=T...]
    all_to_all x1, waiting for transfers between devices: 0.01 us -> 1.99 us  [on_device(): lax.all_to_all(slots, ('oct', 'box'), split_axis=0, concat_axis=0, tiled=...]
  transfers between devices with their start and end apart: 2 -> 2, of which waited for: 1 -> 2; matrix products, arithmetic and copies ran while one was open for 0% -> 0% of each run, Pallas kernels for 41% -> 19%
where the time goes in v1:
time: 64.7 us; the launch traced here: 64.2 us
  Pallas kernels  20.9 us (32%)
  starting transfers between devices  19.3 us (30%)
  waiting for transfers between devices  16.9 us (26%)
  local copies, waits for them, and re-layouts  6.36 us (10%)
  between operations  0.86 us (1%)
    pallas_call x5, Pallas kernels, call(): pl.pallas_call(kernel, out_shape=out_shape, scratch_shapes=scratch, compi...  20.9 us
    all_to_all x1, waiting for transfers between devices, on_device(): lax.all_to_all(sent, ('oct', 'box'), split_axis=0, concat_axis=0, tiled=T...  14.9 us
    all_to_all x1, starting transfers between devices, on_device(): lax.all_to_all(slots, ('oct', 'box'), split_axis=0, concat_axis=0, tiled=...  11.5 us
    all_to_all x1, starting transfers between devices, on_device(): lax.all_to_all(sent, ('oct', 'box'), split_axis=0, concat_axis=0, tiled=T...  7.79 us
    unnamed x42, local copies, waits for them, and re-layouts  6.36 us
    all_to_all x1, waiting for transfers between devices, on_device(): lax.all_to_all(slots, ('oct', 'box'), split_axis=0, concat_axis=0, tiled=...  1.99 us
  transfers between devices with their start and end apart: 2, of which 2 were waited for; matrix products, arithmetic and copies ran while one was open for 0% of the time, Pallas kernels for 19%

profile of v1, /device:TPU:1, one launch (start us, length us, event | category | flops | bytes accessed | tf_op | source)
XLA Modules:
  0.0 64.2 jit_solution(5327113638205935546)
XLA Ops:
  0.6 0.0 copy-start.7
  0.6 0.7 %copy-done.7 = s32[2048,2]{0,1:T(2,128)S(1)} copy-done((s32[2048,2]{0,1:T(2,128)S(1)}, s32[2048,2]{0,1:T(2,128)}, u32[]{:S(2)}) %copy-start.7) | copy-done | bytes 16408
  1.4 0.0 copy-start.11
  1.4 0.7 %copy-done.11 = s32[2048,1]{0,1:T(1,128)S(1)} copy-done((s32[2048,1]{0,1:T(1,128)S(1)}, s32[2048,1]{0,1:T(1,128)}, u32[]{:S(2)}) %copy-start.11) | copy-done | bytes 8216
  2.0 0.0 copy-start.14
  2.1 0.7 %copy-done.14 = s32[512,2]{0,1:T(2,128)S(1)} copy-done((s32[512,2]{0,1:T(2,128)S(1)}, s32[512,2]{0,1:T(2,128)}, u32[]{:S(2)}) %copy-start.14) | copy-done | bytes 4120
  2.7 0.0 copy-start.17
  2.7 0.7 %copy-done.17 = s32[512,1]{0,1:T(1,128)S(1)} copy-done((s32[512,1]{0,1:T(1,128)S(1)}, s32[512,1]{0,1:T(1,128)}, u32[]{:S(2)}) %copy-start.17) | copy-done | bytes 2072
  3.4 0.0 copy-start.2
  3.4 0.0 copy-start.4
  3.4 0.0 copy-start.6
  3.4 0.0 copy-start.8
  3.4 0.0 copy-start.9
  3.4 0.0 copy-start.12
  3.5 0.0 copy-start.13
  3.5 0.0 copy-start.15
  3.5 0.0 copy-start.16
  3.5 0.0 copy-start.18
  3.5 1.7 %shard_map.158 = (s32[128,1,128]{2,1,0:T(1,128)}, s32[1,2048]{1,0:T(1,128)S(1)}, s32[1,512]{1,0:T(1,128)S(1)}) custom-call(s32[1,2048]{1,0:T(1,128)S(1)} %bitcast.19, s32[2,2048]{1,0:T(2,128)S(1)} %bitcast.14, s32[1,512]{1,0:T(1,128)S(1)} %bitcast.27, s32[2,512]{1,0:T(2,128)S(1)} %bitcast.23), custom_call_target="tpu_custom_call" | custom-call | flops 1000000000 | bytes 1000000 | tf_op jit(solution)/shard_map/pallas_call | solution.py:308
  5.1 11.5 %all-to-all-start = ((s32[128,1,128]{2,1,0:T(1,128)}), s32[128,1,128]{2,1,0:T(1,128)S(1)}, u32[]{:S(2)}, u32[]{:S(2)}) async-start(s32[128,1,128]{2,1,0:T(1,128)} %get-tuple-element.9), calls=%async_computation | async-start | bytes 131072 | tf_op jit(solution)/shard_map/all_to_all | solution.py:350
  16.7 0.0 copy-done.2
  16.7 0.0 copy-done.4
  16.7 0.0 copy-done.6
  16.7 0.0 copy-done.8
  16.7 0.0 copy-done.9
  16.7 0.0 copy-done.12
  16.7 0.0 copy-done.13
  16.7 0.0 copy-done.15
  16.7 0.0 copy-done.16
  16.7 0.0 copy-done.18
  16.8 0.0 copy-start
  16.8 1.9 %copy-done = bf16[316,64,64]{0,2,1:T(8,128)(2,1)S(1)} copy-done((bf16[316,64,64]{0,2,1:T(8,128)(2,1)S(1)}, bf16[316,64,64]{0,2,1:T(8,128)(2,1)}, u32[]{:S(2)}) %copy-start) | copy-done | bytes 2588696
  18.6 5.4 %shard_map.159 = (bf16[96,64,64]{2,1,0:T(8,128)(2,1)S(1)}, bf16[128,20,128]{2,1,0:T(8,128)(2,1)S(1)}) custom-call(bf16[64,64,316]{2,1,0:T(8,128)(2,1)S(1)} %bitcast.11, s32[64,128]{1,0:T(8,128)S(1)} %bitcast.13, s32[16,128]{1,0:T(8,128)S(1)} %bitcast.17, s32[8,128]{1,0:T(8,128)S(1)} %bitcast.22, s32[4,128]{1,0:T(4,128)S(1)} %bitcast.26, ...), custom_call_target="tpu_custom_call" | custom-call | flops 5000000000 | bytes 10000000 | tf_op jit(solution)/shard_map/pallas_call | solution.py:308
  24.1 2.0 %all-to-all-done.slots = s32[128,1,128]{2,1,0:T(1,128)S(1)} async-done(((s32[128,1,128]{2,1,0:T(1,128)}), s32[128,1,128]{2,1,0:T(1,128)S(1)}, u32[]{:S(2)}, u32[]{:S(2)}) %all-to-all-start) | async-done | bytes 65568 | tf_op jit(solution)/shard_map/all_to_all | solution.py:350
  26.1 2.0 %shard_map.160 = bf16[128,40,128]{2,1,0:T(8,128)(2,1)} custom-call(s32[128,1,128]{2,1,0:T(1,128)S(1)} %all-to-all-done.slots, bf16[64,512]{1,0:T(8,128)(2,1)S(1)} %copy-done.2, bf16[64,64]{1,0:T(8,128)(2,1)S(1)} %copy-done.6, bf16[128,20,128]{2,1,0:T(8,128)(2,1)S(1)} %get-tuple-element.12.part), custom_call_target="tpu_custom_call" | custom-call | flops 1000000000 | bytes 1000000 | tf_op jit(solution)/shard_map/pallas_call | solution.py:308
  28.0 0.0 copy-start.3
  28.0 0.0 copy-start.10
  28.0 7.8 %all-to-all-start.1 = ((bf16[128,40,128]{2,1,0:T(8,128)(2,1)}), bf16[128,40,128]{2,1,0:T(8,128)(2,1)S(1)}, u32[]{:S(2)}, u32[]{:S(2)}) async-start(bf16[128,40,128]{2,1,0:T(8,128)(2,1)} %shard_map.160), calls=%async_computation.1 | async-start | bytes 2621440 | tf_op jit(solution)/shard_map/all_to_all | solution.py:379
  35.8 0.0 copy-done.3
  35.8 0.0 copy-done.10
  35.9 0.0 copy-start.1
  35.9 0.0 copy-start.5
  35.9 6.5 %shard_map.161 = (f32[256,256]{1,0:T(8,128)S(1)}, f32[128,64]{1,0:T(8,128)S(1)}) custom-call(bf16[96,64,64]{2,1,0:T(8,128)(2,1)S(1)} %get-tuple-element.13.sel, bf16[64,512]{1,0:T(8,128)(2,1)S(1)} %copy-done.2, bf16[64,64]{1,0:T(8,128)(2,1)S(1)} %copy-done.6, s32[2,8192]{1,0:T(2,128)S(1)} %bitcast.12, s32[2,1024]{1,0:T(2,128)S(1)} %bitcast.18), custom_call_target="tpu_custom_call" | custom-call | flops 10000000000 | bytes 10000000 | tf_op jit(solution)/shard_map/pallas_call | solution.py:308
  42.4 0.0 copy-start.19
  42.4 0.7 %copy-done.19 = f32[256,256]{1,0:T(8,128)} copy-done((f32[256,256]{1,0:T(8,128)}, f32[256,256]{1,0:T(8,128)S(1)}, u32[]{:S(2)}) %copy-start.19) | copy-done | bytes 262168
  43.1 14.9 %all-to-all-done.1.got = bf16[128,40,128]{2,1,0:T(8,128)(2,1)S(1)} async-done(((bf16[128,40,128]{2,1,0:T(8,128)(2,1)}), bf16[128,40,128]{2,1,0:T(8,128)(2,1)S(1)}, u32[]{:S(2)}, u32[]{:S(2)}) %all-to-all-start.1) | async-done | bytes 1310752 | tf_op jit(solution)/shard_map/all_to_all | solution.py:379
  58.0 0.0 copy-done.1
  58.0 0.0 copy-done.5
  58.0 0.0 copy-start.20
  58.0 0.9 %copy-done.20 = f32[256,256]{1,0:T(8,128)S(1)} copy-done((f32[256,256]{1,0:T(8,128)S(1)}, f32[256,256]{1,0:T(8,128)}, u32[]{:S(2)}) %copy-start.20) | copy-done | bytes 262168
  58.9 5.3 %shard_map.162 = (bf16[64,64]{1,0:T(8,128)(2,1)}, bf16[64,512]{1,0:T(8,128)(2,1)}) custom-call(bf16[128,40,128]{2,1,0:T(8,128)(2,1)S(1)} %all-to-all-done.1.got, s32[128,1,128]{2,1,0:T(1,128)S(1)} %all-to-all-done.slots, bf16[96,64,64]{2,1,0:T(8,128)(2,1)S(1)} %get-tuple-element.13.sel, f32[256,256]{1,0:T(8,128)S(1)} %copy-done.20, ...), custom_call_target="tpu_custom_call" | custom-call | flops 3000000000 | bytes 10000000 | tf_op jit(solution)/shard_map/pallas_call | solution.py:308
Async XLA Ops:
  0.6 0.7 %copy-start.7 = (s32[2048,2]{0,1:T(2,128)S(1)}, s32[2048,2]{0,1:T(2,128)}, u32[]{:S(2)}) copy-start(s32[2048,2]{0,1:T(2,128)} %param.27) | copy-start | bytes 49156
  1.4 0.7 %copy-start.11 = (s32[2048,1]{0,1:T(1,128)S(1)}, s32[2048,1]{0,1:T(1,128)}, u32[]{:S(2)}) copy-start(s32[2048,1]{0,1:T(1,128)} %param.28) | copy-start | bytes 24580
  2.0 0.7 %copy-start.14 = (s32[512,2]{0,1:T(2,128)S(1)}, s32[512,2]{0,1:T(2,128)}, u32[]{:S(2)}) copy-start(s32[512,2]{0,1:T(2,128)} %param.22) | copy-start | bytes 12292
  2.7 0.7 %copy-start.17 = (s32[512,1]{0,1:T(1,128)S(1)}, s32[512,1]{0,1:T(1,128)}, u32[]{:S(2)}) copy-start(s32[512,1]{0,1:T(1,128)} %param.23) | copy-start | bytes 6148
  3.4 13.2 %copy-start.2 = (bf16[64,512]{1,0:T(8,128)(2,1)S(1)}, bf16[64,512]{1,0:T(8,128)(2,1)}, u32[]{:S(2)}) copy-start(bf16[64,512]{1,0:T(8,128)(2,1)} %fm.5) | copy-start | bytes 196612
  3.4 13.2 %copy-start.4 = (s32[8192]{0:T(1024)S(1)}, s32[8192]{0:T(1024)}, u32[]{:S(2)}) copy-start(s32[8192]{0:T(1024)} %param.26) | copy-start | bytes 98308
  3.4 13.3 %copy-start.6 = (bf16[64,64]{1,0:T(8,128)(2,1)S(1)}, bf16[64,64]{1,0:T(8,128)(2,1)}, u32[]{:S(2)}) copy-start(bf16[64,64]{1,0:T(8,128)(2,1)} %cm.5) | copy-start | bytes 24580
  3.4 13.3 %copy-start.8 = (s32[2048,2]{0,1:T(2,128)S(1)}, s32[2048,2]{0,1:T(2,128)}, u32[]{:S(2)}) copy-start(s32[2048,2]{0,1:T(2,128)} %param.27) | copy-start | bytes 49156
  3.4 13.3 %copy-start.9 = (s32[2048]{0:T(1024)S(1)}, s32[2048]{0:T(1024)}, u32[]{:S(2)}) copy-start(s32[2048]{0:T(1024)} %param.29) | copy-start | bytes 24580
  3.4 13.3 %copy-start.12 = (s32[2048,1]{0,1:T(1,128)S(1)}, s32[2048,1]{0,1:T(1,128)}, u32[]{:S(2)}) copy-start(s32[2048,1]{0,1:T(1,128)} %param.28) | copy-start | bytes 24580
  3.5 13.3 %copy-start.13 = (s32[1024]{0:T(1024)S(1)}, s32[1024]{0:T(1024)}, u32[]{:S(2)}) copy-start(s32[1024]{0:T(1024)} %param.21) | copy-start | bytes 12292
  3.5 13.3 %copy-start.15 = (s32[512,2]{0,1:T(2,128)S(1)}, s32[512,2]{0,1:T(2,128)}, u32[]{:S(2)}) copy-start(s32[512,2]{0,1:T(2,128)} %param.22) | copy-start | bytes 12292
  3.5 13.3 %copy-start.16 = (s32[512]{0:T(512)S(1)}, s32[512]{0:T(512)}, u32[]{:S(2)}) copy-start(s32[512]{0:T(512)} %param.24) | copy-start | bytes 6148
  3.5 13.3 %copy-start.18 = (s32[512,1]{0,1:T(1,128)S(1)}, s32[512,1]{0,1:T(1,128)}, u32[]{:S(2)}) copy-start(s32[512,1]{0,1:T(1,128)} %param.23) | copy-start | bytes 6148
  5.1 20.9 %all-to-all-start = ((s32[128,1,128]{2,1,0:T(1,128)}), s32[128,1,128]{2,1,0:T(1,128)S(1)}, u32[]{:S(2)}, u32[]{:S(2)}) async-start(s32[128,1,128]{2,1,0:T(1,128)} %get-tuple-element.9), calls=%async_computation | async-start | bytes 131072 | tf_op jit(solution)/shard_map/all_to_all | solution.py:350
  16.8 1.9 %copy-start = (bf16[316,64,64]{0,2,1:T(8,128)(2,1)S(1)}, bf16[316,64,64]{0,2,1:T(8,128)(2,1)}, u32[]{:S(2)}) copy-start(bf16[316,64,64]{0,2,1:T(8,128)(2,1)} %param.18) | copy-start | bytes 7766020
  28.0 7.8 %copy-start.3 = (s32[8192,2]{0,1:T(2,128)S(1)}, s32[8192,2]{0,1:T(2,128)}, u32[]{:S(2)}) copy-start(s32[8192,2]{0,1:T(2,128)} %param.25) | copy-start | bytes 196612
  28.0 7.8 %copy-start.10 = (s32[1024,2]{0,1:T(2,128)S(1)}, s32[1024,2]{0,1:T(2,128)}, u32[]{:S(2)}) copy-start(s32[1024,2]{0,1:T(2,128)} %param.20) | copy-start | bytes 24580
  28.0 29.9 %all-to-all-start.1 = ((bf16[128,40,128]{2,1,0:T(8,128)(2,1)}), bf16[128,40,128]{2,1,0:T(8,128)(2,1)S(1)}, u32[]{:S(2)}, u32[]{:S(2)}) async-start(bf16[128,40,128]{2,1,0:T(8,128)(2,1)} %shard_map.160), calls=%async_computation.1 | async-start | bytes 2621440 | tf_op jit(solution)/shard_map/all_to_all | solution.py:379
  35.9 22.1 %copy-start.1 = (bf16[8,64,64]{2,1,0:T(8,128)(2,1)S(1)}, bf16[8,64,64]{2,1,0:T(8,128)(2,1)}, u32[]{:S(2)}) copy-start(bf16[8,64,64]{2,1,0:T(8,128)(2,1)} %maps.1) | copy-start | bytes 196612
  35.9 22.1 %copy-start.5 = (f32[64,64]{1,0:T(8,128)S(1)}, f32[64,64]{1,0:T(8,128)}, u32[]{:S(2)}) copy-start(f32[64,64]{1,0:T(8,128)} %parent.1) | copy-start | bytes 49156
  42.4 0.7 %copy-start.19 = (f32[256,256]{1,0:T(8,128)}, f32[256,256]{1,0:T(8,128)S(1)}, u32[]{:S(2)}) copy-start(f32[256,256]{1,0:T(8,128)S(1)} %get-tuple-element.14.f_near) | copy-start | bytes 786436
  58.0 1.0 %copy-start.20 = (f32[256,256]{1,0:T(8,128)S(1)}, f32[256,256]{1,0:T(8,128)}, u32[]{:S(2)}) copy-start(f32[256,256]{1,0:T(8,128)} %copy-done.19) | copy-start | bytes 786436

commit v2 on v1

v2 whole, which is shorter than its diff:
```python
import jax
import jax.numpy as jnp
from jax import lax
from jax.experimental import pallas as pl
from jax.experimental.pallas import tpu as pltpu
from jax.sharding import PartitionSpec as P


F32 = jnp.float32
BF16 = jnp.bfloat16
I32 = jnp.int32

DEV = 128
RANK = 64
CAP_F = 32
CAP_C = 8
ROWS_F = CAP_F * RANK // 128
ROWS_C = CAP_C * RANK // 128
ROWS = 2 * (ROWS_F + ROWS_C)
HALF_CAP = CAP_F // 2
PART_CAP = CAP_F // 4
G_NEAR_F, G_FAR_F, G_NEAR_C, G_FAR_C = 64, 16, 8, 4
FAR_GROUPS = 24
NEAR_GROUPS = G_NEAR_F + G_NEAR_C
NEAR_BLOCK = 4096
PM_ROWS = 512
MIB_1, MIB_2, MIB_3, MIB_4, MIB_5 = 60, 32, 24, 40, 40


def mm(a, b):
    return lax.dot_general(a, b, (((1,), (0,)), ((), ())), preferred_element_type=F32)


def mm_nt(a, b):
    return lax.dot_general(a, b, (((1,), (1,)), ((), ())), preferred_element_type=F32)


def mm_tn(a, b):
    return lax.dot_general(a, b, (((0,), (0,)), ((), ())), preferred_element_type=F32)


def one_hot(row, count):
    n = row.shape[1]
    at = lax.broadcasted_iota(I32, (count, n), 0).astype(BF16)
    hit = at == jnp.broadcast_to(row.astype(BF16), (count, n))
    return jnp.where(hit, jnp.ones((), BF16), jnp.zeros((), BF16))


def one_hot_wide(row, count):
    return jnp.concatenate(
        [one_hot(jnp.clip(row - at, -1, 256), 256) for at in range(0, count, 256)], axis=0
    )


def half_stack(m):
    return jnp.concatenate([m[:, :256], m[:, 256:]], axis=0)


def pick_fine(stack, hot, row):
    both = mm(stack, hot)
    return jnp.where(row < 256, both[:RANK], both[RANK:])


def split_rows(values):
    high = values.astype(BF16)
    low = (values - high.astype(F32)).astype(BF16)
    return jnp.concatenate([high, low], axis=0)


def spread_fine(values, row):
    first = jnp.where(row < 256, values, 0.0)
    second = jnp.where(row < 256, 0.0, values)
    return split_rows(jnp.concatenate([first, second], axis=0))


def prefix_matrix():
    down = lax.broadcasted_iota(I32, (128, 256), 0)
    across = lax.broadcasted_iota(I32, (128, 256), 1)
    return jnp.where((down <= across) | (across >= 128), 1.0, 0.0).astype(BF16)


def fetch(pairs, sems):
    copies = [pltpu.make_async_copy(a, b, sems.at[i]) for i, (a, b) in enumerate(pairs)]
    for copy in copies:
        copy.start()
    for copy in copies:
        copy.wait()


def route_kernel(
    f_owner_in, f_boxes_in, c_owner_in, c_boxes_in, slots_ref, f_pos, c_pos,
    f_owner, f_boxes, c_owner, c_boxes, sems,
):
    fetch(
        [(f_owner_in, f_owner), (f_boxes_in, f_boxes), (c_owner_in, c_owner), (c_boxes_in, c_boxes)],
        sems,
    )
    f_blocks, c_blocks = f_owner.shape[1] // 128, c_owner.shape[1] // 128
    hits = [
        lax.broadcasted_iota(I32, (DEV, 128), 0) == ref[:, b * 128:(b + 1) * 128]
        for ref, blocks in ((f_owner, f_blocks), (c_owner, c_blocks))
        for b in range(blocks)
    ]
    hots = [jnp.where(hit, 1.0, 0.0).astype(BF16) for hit in hits]
    counts = mm(jnp.concatenate(hots, axis=0), prefix_matrix())

    def place(boxes_ref, pos_ref, start, blocks, cap, wide):
        carry = jnp.zeros((DEV, 128), F32)
        parts = []
        for b in range(blocks):
            lanes = slice(b * 128, (b + 1) * 128)
            count = counts[(start + b) * 128:(start + b + 1) * 128]
            seen = count[:, :128] + carry
            pos = jnp.sum(jnp.where(hits[start + b], seen, 0.0), axis=0, keepdims=True) - 1.0
            carry = carry + count[:, 128:]
            pos = pos.astype(I32)
            pos_ref[:, lanes] = pos
            slot = boxes_ref[1:2, lanes]
            here = lax.broadcasted_iota(I32, (cap, 128), 0) == pos
            low = jnp.where(here, (slot & 255).astype(F32), 0.0)
            if wide:
                high = jnp.where(here, (slot >> 8).astype(F32), 0.0)
                low = jnp.concatenate([low, high], axis=0)
            parts.append(low.astype(BF16))
        table = mm_nt(
            jnp.concatenate(parts, axis=1), jnp.concatenate(hots[start:start + blocks], axis=1)
        )
        if wide:
            table = table[:cap] + 256.0 * table[cap:]
        return table

    fine = place(f_boxes, f_pos, 0, f_blocks, CAP_F, True)
    coarse = place(c_boxes, c_pos, f_blocks, c_blocks, CAP_C, False)
    rest = jnp.zeros((128 - CAP_F - CAP_C, DEV), F32)
    table = jnp.concatenate([fine, coarse, rest], axis=0)
    slots_ref[:, 0, :] = jnp.transpose(table).astype(I32)


def pick_operators(ops, kinds, flat, out):
    groups, nt = kinds.shape[0], ops.shape[2]
    hot = jnp.where(kinds[:, 0:1] == lax.broadcasted_iota(I32, (groups, nt), 1), 1.0, 0.0)
    hot = hot.astype(BF16)
    for quad in range(RANK // 4):
        rows = ops[quad * 4:(quad + 1) * 4].reshape(256, nt)
        got = mm_nt(hot, rows)
        for k in range(4):
            flat[pl.ds(quad * 4 + k, groups, stride=RANK), :] = got[:, k * RANK:(k + 1) * RANK]
    out[...] = flat[...].reshape(groups, RANK, RANK).astype(BF16)


def outgoing_kernel(
    ops, s_ff, s_fc, fm, cm, f_owner, f_boxes, f_pos, c_owner, c_boxes, c_pos,
    sel_ref, f_part, c_part, kinds, kf, pm, hot_out, flat,
):
    kinds[...] = jnp.zeros_like(kinds)
    kinds[0:G_FAR_F] = s_ff[...]
    kinds[G_FAR_F:G_FAR_F + G_FAR_C] = s_fc[...]
    pick_operators(ops, kinds, kf, sel_ref)

    row = c_boxes[0:1, :]
    vec = mm(cm[...], one_hot(row, 64)).astype(BF16)
    part = jnp.concatenate(
        [
            mm_tn(sel_ref[G_FAR_F + g], vec[:, g * 128:(g + 1) * 128])
            for g in range(G_FAR_C)
        ],
        axis=1,
    )
    pos = c_pos[...]
    pieces = [jnp.where(pos == k, part, 0.0).astype(BF16) for k in range(CAP_C)]
    big = mm_nt(jnp.concatenate(pieces, axis=0), one_hot(c_owner[...], DEV))
    for kp in range(ROWS_C):
        c_part[kp] = jnp.transpose(big[kp * 128:(kp + 1) * 128])

    stack = half_stack(fm[...])
    row = f_boxes[0:1, :]
    vec = pick_fine(stack, one_hot(row & 255, 256), row).astype(BF16)
    part = jnp.concatenate(
        [
            mm_tn(sel_ref[g], vec[:, g * 128:(g + 1) * 128])
            for g in range(G_FAR_F)
        ],
        axis=1,
    )
    part = (2.0 * part).astype(BF16)
    pos = f_pos[...]
    hot_out[...] = one_hot((pos >> 4) * DEV + f_owner[...], 2 * DEV)
    step = jnp.broadcast_to((pos & (HALF_CAP - 1)).astype(BF16), part.shape)
    none = jnp.zeros((), BF16)
    for k in range(HALF_CAP):
        pm[k * RANK:(k + 1) * RANK, :] = jnp.where(step == jnp.asarray(k, BF16), part, none)
    for j in range(HALF_CAP * RANK // PM_ROWS):
        big = mm_nt(pm[j * PM_ROWS:(j + 1) * PM_ROWS, :], hot_out[...])
        for i in range(PM_ROWS // 128):
            kp = j * (PM_ROWS // 128) + i
            for half in range(2):
                turned = jnp.transpose(big[i * 128:(i + 1) * 128, half * DEV:(half + 1) * DEV])
                flat[pl.ds(half * (HALF_CAP // 2) + kp, DEV, stride=ROWS_F), :] = turned

    f_part[...] = flat[...].reshape(DEV, ROWS_F, 128).astype(BF16)


def slot_rows(slots):
    table = jnp.transpose(slots[:, 0, :].astype(F32)).astype(I32)
    rows = [table[k:k + 1] for k in range(CAP_F + CAP_C)]
    return jnp.concatenate(rows[:CAP_F], axis=1), jnp.concatenate(rows[CAP_F:], axis=1)


def reply_kernel(slots, fm, cm, f_part, c_part, out_ref, f_flat, c_flat):
    f_row, c_row = slot_rows(slots)
    f_vec = pick_fine(half_stack(fm[...]), one_hot(f_row & 255, 256), f_row)
    c_vec = mm(cm[...], one_hot(c_row, 64))

    def turned(vec, kp):
        at = 2 * kp * DEV
        return jnp.transpose(
            jnp.concatenate([vec[:, at:at + DEV], vec[:, at + DEV:at + 2 * DEV]], axis=0)
        )

    for kp in range(ROWS_F):
        f_flat[pl.ds(kp, DEV, stride=ROWS_F), :] = turned(f_vec, kp)
    for kp in range(ROWS_C):
        c_flat[pl.ds(kp, DEV, stride=2 * ROWS_C), :] = turned(c_vec, kp)
        c_flat[pl.ds(ROWS_C + kp, DEV, stride=2 * ROWS_C), :] = c_part[kp]
    out_ref[...] = jnp.concatenate(
        [
            f_flat[...].reshape(DEV, ROWS_F, 128).astype(BF16),
            f_part[...],
            c_flat[...].reshape(DEV, 2 * ROWS_C, 128).astype(BF16),
        ],
        axis=1,
    )


def near_kernel(ops, s_nf, s_nc, fm, cm, f_boxes, c_boxes, f_out, c_out, kinds, kf, sel, f_sum):
    kinds[0:G_NEAR_F] = s_nf[...]
    kinds[G_NEAR_F:NEAR_GROUPS] = s_nc[...]
    pick_operators(ops, kinds, kf, sel)
    stack = half_stack(fm[...])
    f_sum[...] = jnp.zeros_like(f_sum)

    def step(i, carry):
        lanes = pl.ds(pl.multiple_of(i * NEAR_BLOCK, NEAR_BLOCK), NEAR_BLOCK)
        first = f_boxes[0:1, lanes]
        second = f_boxes[1:2, lanes]
        hot_1 = one_hot(first & 255, 256)
        hot_2 = one_hot(second & 255, 256)
        vec_1 = pick_fine(stack, hot_1, first).astype(BF16)
        vec_2 = pick_fine(stack, hot_2, second).astype(BF16)
        to_1, to_2 = [], []
        for k in range(NEAR_BLOCK // 128):
            op = sel[NEAR_BLOCK // 128 * i + k]
            cut = slice(k * 128, (k + 1) * 128)
            to_1.append(mm(op, vec_2[:, cut]))
            to_2.append(mm_tn(op, vec_1[:, cut]))
        to_1 = jnp.concatenate(to_1, axis=1)
        to_2 = jnp.concatenate(to_2, axis=1)
        both = jnp.concatenate([spread_fine(to_1, first), spread_fine(to_2, second)], axis=1)
        hots = jnp.concatenate([hot_1, hot_2], axis=1)
        f_sum[...] += mm_nt(both, hots)
        return carry

    lax.fori_loop(0, G_NEAR_F * 128 // NEAR_BLOCK, step, 0)
    f_out[...] = f_sum[:2 * RANK] + f_sum[2 * RANK:]
    total = jnp.zeros((2 * RANK, 64), F32)
    for g in range(G_NEAR_C):
        lanes = slice(g * 128, (g + 1) * 128)
        hot_1 = one_hot(c_boxes[0:1, lanes], 64)
        hot_2 = one_hot(c_boxes[1:2, lanes], 64)
        vec_1 = mm(cm[...], hot_1).astype(BF16)
        vec_2 = mm(cm[...], hot_2).astype(BF16)
        op = sel[G_NEAR_F + g]
        total = total + mm_nt(split_rows(mm(op, vec_2)), hot_1)
        total = total + mm_nt(split_rows(mm_tn(op, vec_1)), hot_2)
    c_out[...] = total[:RANK] + total[RANK:]


def final_kernel(
    got, slots, sel, f_near, c_near, parent, maps, f_owner, f_boxes, f_pos, c_owner, c_boxes, c_pos,
    c_ref, f_ref, flat,
):
    flat[...] = got[...].astype(F32).reshape(DEV * ROWS, 128)
    f_row, c_row = slot_rows(slots)

    def turned(row):
        return jnp.transpose(flat[pl.ds(row, DEV, stride=ROWS), :])

    def choose(found, where, count):
        vec = found[:RANK]
        for k in range(1, count):
            vec = jnp.where(where == k, found[k * RANK:(k + 1) * RANK], vec)
        return vec.astype(BF16)

    held_c = jnp.concatenate([turned(2 * ROWS_F + kp) for kp in range(ROWS_C)], axis=0)
    vec_c = choose(mm(held_c.astype(BF16), one_hot(c_owner[...], DEV)), c_pos[...], CAP_C)
    to_1 = jnp.concatenate(
        [mm(sel[G_FAR_F + g], vec_c[:, g * 128:(g + 1) * 128]) for g in range(G_FAR_C)], axis=1
    )
    far_c = mm_nt(split_rows(to_1), one_hot(c_boxes[0:1, :], 64))
    sides_c = []
    for kp in range(ROWS_C):
        arrived = turned(2 * ROWS_F + ROWS_C + kp)
        sides_c += [arrived[:RANK], arrived[RANK:]]
    arrived_c = mm_nt(jnp.concatenate(sides_c, axis=1).astype(BF16), one_hot(c_row, 64))
    coarse = parent[...] + c_near[...] + far_c[:RANK] + far_c[RANK:] + arrived_c
    coarse = coarse.astype(BF16)
    c_ref[...] = coarse

    held = jnp.concatenate(
        [
            jnp.concatenate([turned(quarter * (ROWS_F // 4) + kp) for quarter in range(4)], axis=1)
            for kp in range(ROWS_F // 4)
        ],
        axis=0,
    ).astype(BF16)
    pos = f_pos[...]
    hot = one_hot_wide((pos // PART_CAP) * DEV + f_owner[...], 4 * DEV)
    vec = choose(mm(held, hot), pos & (PART_CAP - 1), PART_CAP)
    to_1 = jnp.concatenate(
        [mm(sel[g], vec[:, g * 128:(g + 1) * 128]) for g in range(G_FAR_F)], axis=1
    )
    first = f_boxes[0:1, :]
    total = mm_nt(spread_fine(to_1, first), one_hot(first & 255, 256))
    sides = []
    for kp in range(ROWS_F):
        arrived = turned(ROWS_F + kp)
        sides += [arrived[:RANK], arrived[RANK:]]
    side = jnp.concatenate(sides, axis=1)
    side = jnp.concatenate(
        [jnp.where(f_row < 256, side, 0.0), jnp.where(f_row < 256, 0.0, side)], axis=0
    )
    added = mm_nt(side.astype(BF16), one_hot(f_row & 255, 256))

    box = lax.broadcasted_iota(I32, (64, 512), 1)
    parent_of = jnp.where((box >> 3) == lax.broadcasted_iota(I32, (64, 512), 0), 1.0, 0.0)
    wide = mm(coarse, parent_of.astype(BF16)).astype(BF16)
    starts = mm(maps[...].reshape(8 * RANK, RANK), wide)
    start = starts[:RANK]
    for k in range(1, 8):
        start = jnp.where((box & 7) == k, starts[k * RANK:(k + 1) * RANK], start)

    total = 2.0 * (f_near[...] + total[:2 * RANK] + total[2 * RANK:]) + added
    fine = start + jnp.concatenate([total[:RANK], total[RANK:]], axis=1)
    f_ref[...] = fine.astype(BF16)


def call(kernel, out_shape, scratch, mib, flops, nbytes, *args, **more):
    return pl.pallas_call(
        kernel,
        out_shape=out_shape,
        scratch_shapes=scratch,
        compiler_params=pltpu.CompilerParams(vmem_limit_bytes=mib * 1024 * 1024),
        cost_estimate=pl.CostEstimate(flops=flops, bytes_accessed=nbytes, transcendentals=0),
        **more,
    )(*args)


def on_device(
    coarse_multipole,
    fine_multipole,
    parent_local,
    operators,
    child_maps,
    coarse_near_boxes,
    coarse_near_shift,
    coarse_far_boxes,
    coarse_far_owner,
    coarse_far_shift,
    fine_near_boxes,
    fine_near_shift,
    fine_far_boxes,
    fine_far_owner,
    fine_far_shift,
):
    def sds(shape, dtype):
        return jax.ShapeDtypeStruct(shape, dtype)

    fm, cm = fine_multipole, coarse_multipole
    f_owner, c_owner = fine_far_owner.T, coarse_far_owner.T
    f_far, c_far = fine_far_boxes.T, coarse_far_boxes.T
    ops = jnp.transpose(operators, (1, 2, 0))

    n_f, n_c = f_owner.shape[1], c_owner.shape[1]
    slots, f_pos, c_pos = call(
        route_kernel,
        (sds((DEV, 1, 128), I32), sds((1, n_f), I32), sds((1, n_c), I32)),
        [
            pltpu.VMEM((1, n_f), I32),
            pltpu.VMEM((2, n_f), I32),
            pltpu.VMEM((1, n_c), I32),
            pltpu.VMEM((2, n_c), I32),
            pltpu.SemaphoreType.DMA((4,)),
        ],
        MIB_1,
        10**9,
        10**6,
        f_owner, f_far, c_owner, c_far,
        in_specs=[pl.BlockSpec(memory_space=pltpu.HBM)] * 4,
    )
    asked = lax.all_to_all(slots, ("oct", "box"), split_axis=0, concat_axis=0, tiled=True)
    sel, f_part, c_part = call(
        outgoing_kernel,
        (
            sds((FAR_GROUPS, RANK, RANK), BF16),
            sds((DEV, ROWS_F, 128), BF16),
            sds((ROWS_C, DEV, 128), F32),
        ),
        [
            pltpu.VMEM((FAR_GROUPS, 128), I32),
            pltpu.VMEM((FAR_GROUPS * RANK, RANK), F32),
            pltpu.VMEM((HALF_CAP * RANK, n_f), BF16),
            pltpu.VMEM((2 * DEV, n_f), BF16),
            pltpu.VMEM((DEV * ROWS_F, 128), F32),
        ],
        MIB_2,
        5 * 10**9,
        10**7,
        ops,
        fine_far_shift.reshape(-1, 128),
        coarse_far_shift.reshape(-1, 128),
        fm, cm, f_owner, f_far, f_pos, c_owner, c_far, c_pos,
    )
    sent = call(
        reply_kernel,
        sds((DEV, ROWS, 128), BF16),
        [pltpu.VMEM((DEV * ROWS_F, 128), F32), pltpu.VMEM((DEV * 2 * ROWS_C, 128), F32)],
        MIB_3,
        10**9,
        10**6,
        asked, fm, cm, f_part, c_part,
    )
    got = lax.all_to_all(sent, ("oct", "box"), split_axis=0, concat_axis=0, tiled=True)
    f_near, c_near = call(
        near_kernel,
        (sds((2 * RANK, 256), F32), sds((RANK, 64), F32)),
        [
            pltpu.VMEM((NEAR_GROUPS, 128), I32),
            pltpu.VMEM((NEAR_GROUPS * RANK, RANK), F32),
            pltpu.VMEM((NEAR_GROUPS, RANK, RANK), BF16),
            pltpu.VMEM((4 * RANK, 256), F32),
        ],
        MIB_4,
        10**10,
        10**7,
        ops,
        fine_near_shift.reshape(-1, 128),
        coarse_near_shift.reshape(-1, 128),
        fm, cm, fine_near_boxes.T, coarse_near_boxes.T,
    )
    return call(
        final_kernel,
        (sds((RANK, 64), BF16), sds((RANK, 512), BF16)),
        [pltpu.VMEM((DEV * ROWS, 128), F32)],
        MIB_5,
        3 * 10**9,
        10**7,
        got, asked, sel, f_near, c_near, parent_local, child_maps,
        f_owner, f_far, f_pos, c_owner, c_far, c_pos,
    )


def solution(mesh):
    both = ("oct", "box")
    return jax.shard_map(
        on_device,
        mesh=mesh,
        in_specs=(
            P(None, both),
            P(None, both),
            P(None, both),
            P(),
            P(),
            P(both, None),
            P(both),
            P(both, None),
            P(both, None),
            P(both),
            P(both, None),
            P(both),
            P(both, None),
            P(both, None),
            P(both),
        ),
        out_specs=(P(None, both), P(None, both)),
        check_vma=False,
    )
```

time: 64.7 us -> 60 us (0.927)
  waiting for transfers between devices: 16.9 us -> 14.1 us
  local copies, waits for them, and re-layouts: 6.36 us -> 5.2 us
    all_to_all x1, waiting for transfers between devices: 14.9 us -> 11.6 us  [on_device(): lax.all_to_all(sent, ('oct', 'box'), split_axis=0, concat_axis=0, tiled=T...]
    unnamed x42 -> x40, local copies, waits for them, and re-layouts: 6.36 us -> 5.2 us
  transfers between devices with their start and end apart: 2 -> 2, of which waited for: 2 -> 2; matrix products, arithmetic and copies ran while one was open for 0% -> 0% of each run, Pallas kernels for 19% -> 20%
where the time goes in v2:
time: 60 us; the launch traced here: 59.6 us
  Pallas kernels  20.6 us (34%)
  starting transfers between devices  18.7 us (31%)
  waiting for transfers between devices  14.1 us (24%)
  local copies, waits for them, and re-layouts  5.2 us (9%)
  between operations  0.87 us (1%)
    pallas_call x5, Pallas kernels, call(): pl.pallas_call(kernel, out_shape=out_shape, scratch_shapes=scratch, compi...  20.6 us
    all_to_all x1, waiting for transfers between devices, on_device(): lax.all_to_all(sent, ('oct', 'box'), split_axis=0, concat_axis=0, tiled=T...  11.6 us
    all_to_all x1, starting transfers between devices, on_device(): lax.all_to_all(slots, ('oct', 'box'), split_axis=0, concat_axis=0, tiled=...  11.5 us
    all_to_all x1, starting transfers between devices, on_device(): lax.all_to_all(sent, ('oct', 'box'), split_axis=0, concat_axis=0, tiled=T...  7.22 us
    unnamed x40, local copies, waits for them, and re-layouts  5.2 us
    all_to_all x1, waiting for transfers between devices, on_device(): lax.all_to_all(slots, ('oct', 'box'), split_axis=0, concat_axis=0, tiled=...  2.56 us
  transfers between devices with their start and end apart: 2, of which 2 were waited for; matrix products, arithmetic and copies ran while one was open for 0% of the time, Pallas kernels for 20%

profile of v2, /device:TPU:1, one launch (start us, length us, event | category | flops | bytes accessed | tf_op | source)
XLA Modules:
  0.0 59.6 jit_solution(6133210412399420368)
XLA Ops:
  0.6 0.0 copy-start.3
  0.6 0.0 copy-start.7
  0.7 0.0 copy-start.8
  0.7 0.0 copy-start.9
  0.7 0.0 copy-start.11
  0.7 0.0 copy-start.13
  0.7 0.0 copy-start.14
  0.7 0.0 copy-start.15
  0.7 2.4 %shard_map.158 = (s32[128,1,128]{2,1,0:T(1,128)}, s32[1,2048]{1,0:T(1,128)}, s32[1,512]{1,0:T(1,128)}) custom-call(s32[1,2048]{1,0:T(1,128)} %bitcast.20, s32[2,2048]{1,0:T(2,128)} %bitcast.15, s32[1,512]{1,0:T(1,128)} %bitcast.28, s32[2,512]{1,0:T(2,128)} %bitcast.24), custom_call_target="tpu_custom_call" | custom-call | flops 1000000000 | bytes 1000000 | tf_op jit(solution)/shard_map/pallas_call | solution.py:348
  3.2 11.5 %all-to-all-start = ((s32[128,1,128]{2,1,0:T(1,128)}), s32[128,1,128]{2,1,0:T(1,128)S(1)}, u32[]{:S(2)}, u32[]{:S(2)}) async-start(s32[128,1,128]{2,1,0:T(1,128)} %get-tuple-element.10), calls=%async_computation | async-start | bytes 131072 | tf_op jit(solution)/shard_map/all_to_all | solution.py:400
  14.7 0.0 copy-done.3
  14.7 0.0 copy-done.7
  14.7 0.0 copy-done.8
  14.7 0.0 copy-done.9
  14.7 0.0 copy-done.11
  14.7 0.0 copy-done.13
  14.7 0.0 copy-done.14
  14.7 0.0 copy-done.15
  14.8 0.0 copy-start
  14.8 1.9 %copy-done = bf16[316,64,64]{0,2,1:T(8,128)(2,1)S(1)} copy-done((bf16[316,64,64]{0,2,1:T(8,128)(2,1)S(1)}, bf16[316,64,64]{0,2,1:T(8,128)(2,1)}, u32[]{:S(2)}) %copy-start) | copy-done | bytes 2588696
  16.6 0.0 copy-start.16
  16.6 0.7 %copy-done.16 = s32[1,2048]{1,0:T(1,128)S(1)} copy-done((s32[1,2048]{1,0:T(1,128)S(1)}, s32[1,2048]{1,0:T(1,128)}, u32[]{:S(2)}) %copy-start.16) | copy-done | bytes 8216
  17.3 0.0 copy-start.18
  17.3 0.7 %copy-done.18 = s32[1,512]{1,0:T(1,128)S(1)} copy-done((s32[1,512]{1,0:T(1,128)S(1)}, s32[1,512]{1,0:T(1,128)}, u32[]{:S(2)}) %copy-start.18) | copy-done | bytes 2072
  18.0 3.5 %shard_map.159 = (bf16[24,64,64]{2,1,0:T(8,128)(2,1)S(1)}, bf16[128,16,128]{2,1,0:T(8,128)(2,1)S(1)}, f32[4,128,128]{2,1,0:T(8,128)S(1)}) custom-call(bf16[64,64,316]{2,1,0:T(8,128)(2,1)S(1)} %bitcast.11, s32[16,128]{1,0:T(8,128)S(1)} %bitcast.18, s32[4,128]{1,0:T(4,128)S(1)} %bitcast.27, bf16[64,512]{1,0:T(8,128)(2,1)S(1)} %copy-done.3, ...), custom_call_target="tpu_custom_call" | custom-call | flops 5000000000 | bytes 10000000 | tf_op jit(solution)/shard_map/pallas_call | solution.py:348
  21.5 2.6 %all-to-all-done.slots = s32[128,1,128]{2,1,0:T(1,128)S(1)} async-done(((s32[128,1,128]{2,1,0:T(1,128)}), s32[128,1,128]{2,1,0:T(1,128)S(1)}, u32[]{:S(2)}, u32[]{:S(2)}) %all-to-all-start) | async-done | bytes 65568 | tf_op jit(solution)/shard_map/all_to_all | solution.py:400
  24.1 2.1 %shard_map.160 = bf16[128,40,128]{2,1,0:T(8,128)(2,1)} custom-call(s32[128,1,128]{2,1,0:T(1,128)S(1)} %all-to-all-done.slots, bf16[64,512]{1,0:T(8,128)(2,1)S(1)} %copy-done.3, bf16[64,64]{1,0:T(8,128)(2,1)S(1)} %copy-done.7, bf16[128,16,128]{2,1,0:T(8,128)(2,1)S(1)} %get-tuple-element.13.f_part, f32[4,128,128]{2,1,0:T(8,128)S(1)} %get-tuple-element.14.c_part), custom_call_target="tpu_custom_call" | custom-call | flops 1000000000 | bytes 1000000 | tf_op jit(solution)/shard_map/pallas_call | solution.py:348
  26.2 0.0 copy-start.4
  26.2 0.0 copy-start.5
  26.2 0.0 copy-start.10
  26.2 0.0 copy-start.12
  26.2 7.2 %all-to-all-start.1 = ((bf16[128,40,128]{2,1,0:T(8,128)(2,1)}), bf16[128,40,128]{2,1,0:T(8,128)(2,1)S(1)}, u32[]{:S(2)}, u32[]{:S(2)}) async-start(bf16[128,40,128]{2,1,0:T(8,128)(2,1)} %shard_map.160), calls=%async_computation.1 | async-start | bytes 2621440 | tf_op jit(solution)/shard_map/all_to_all | solution.py:432
  33.4 0.0 copy-done.4
  33.4 0.0 copy-done.5
  33.4 0.0 copy-done.10
  33.4 0.0 copy-done.12
  33.4 0.0 copy-start.1
  33.5 1.9 %copy-done.1 = bf16[316,64,64]{0,2,1:T(8,128)(2,1)S(1)} copy-done((bf16[316,64,64]{0,2,1:T(8,128)(2,1)S(1)}, bf16[316,64,64]{0,2,1:T(8,128)(2,1)}, u32[]{:S(2)}) %copy-start.1) | copy-done | bytes 2588696
  35.3 0.0 copy-start.2
  35.3 0.0 copy-start.6
  35.3 0.0 copy-start.17
  35.3 0.0 copy-start.19
  35.3 8.6 %shard_map.161 = (f32[128,256]{1,0:T(8,128)S(1)}, f32[64,64]{1,0:T(8,128)S(1)}) custom-call(bf16[64,64,316]{2,1,0:T(8,128)(2,1)S(1)} %bitcast.12, s32[64,128]{1,0:T(8,128)S(1)} %bitcast.14, s32[8,128]{1,0:T(8,128)S(1)} %bitcast.23, bf16[64,512]{1,0:T(8,128)(2,1)S(1)} %copy-done.3, bf16[64,64]{1,0:T(8,128)(2,1)S(1)} %copy-done.7, s32[2,8192]{1,0:T(2,128)S(1)} %bitcast.13, ...), custom_call_target="tpu_custom_call" | custom-call | flops 10000000000 | bytes 10000000 | tf_op jit(solution)/shard_map/pallas_call | solution.py:348
  44.0 11.6 %all-to-all-done.1.got = bf16[128,40,128]{2,1,0:T(8,128)(2,1)S(1)} async-done(((bf16[128,40,128]{2,1,0:T(8,128)(2,1)}), bf16[128,40,128]{2,1,0:T(8,128)(2,1)S(1)}, u32[]{:S(2)}, u32[]{:S(2)}) %all-to-all-start.1) | async-done | bytes 1310752 | tf_op jit(solution)/shard_map/all_to_all | solution.py:432
  55.5 0.0 copy-done.2
  55.5 0.0 copy-done.6
  55.6 0.0 copy-done.17
  55.6 0.0 copy-done.19
  55.6 4.0 %shard_map.162 = (bf16[64,64]{1,0:T(8,128)(2,1)}, bf16[64,512]{1,0:T(8,128)(2,1)}) custom-call(bf16[128,40,128]{2,1,0:T(8,128)(2,1)S(1)} %all-to-all-done.1.got, s32[128,1,128]{2,1,0:T(1,128)S(1)} %all-to-all-done.slots, bf16[24,64,64]{2,1,0:T(8,128)(2,1)S(1)} %get-tuple-element.15.sel, f32[128,256]{1,0:T(8,128)S(1)} %get-tuple-element.16.f_near, ...), custom_call_target="tpu_custom_call" | custom-call | flops 3000000000 | bytes 10000000 | tf_op jit(solution)/shard_map/pallas_call | solution.py:348
Async XLA Ops:
  0.6 14.0 %copy-start.3 = (bf16[64,512]{1,0:T(8,128)(2,1)S(1)}, bf16[64,512]{1,0:T(8,128)(2,1)}, u32[]{:S(2)}) copy-start(bf16[64,512]{1,0:T(8,128)(2,1)} %fm.5) | copy-start | bytes 196612
  0.6 14.0 %copy-start.7 = (bf16[64,64]{1,0:T(8,128)(2,1)S(1)}, bf16[64,64]{1,0:T(8,128)(2,1)}, u32[]{:S(2)}) copy-start(bf16[64,64]{1,0:T(8,128)(2,1)} %cm.5) | copy-start | bytes 24580
  0.7 14.0 %copy-start.8 = (s32[2048,2]{0,1:T(2,128)S(1)}, s32[2048,2]{0,1:T(2,128)}, u32[]{:S(2)}) copy-start(s32[2048,2]{0,1:T(2,128)} %param.27) | copy-start | bytes 49156
  0.7 14.0 %copy-start.9 = (s32[2048]{0:T(1024)S(1)}, s32[2048]{0:T(1024)}, u32[]{:S(2)}) copy-start(s32[2048]{0:T(1024)} %param.29) | copy-start | bytes 24580
  0.7 14.0 %copy-start.11 = (s32[2048,1]{0,1:T(1,128)S(1)}, s32[2048,1]{0,1:T(1,128)}, u32[]{:S(2)}) copy-start(s32[2048,1]{0,1:T(1,128)} %param.28) | copy-start | bytes 24580
  0.7 14.0 %copy-start.13 = (s32[512,2]{0,1:T(2,128)S(1)}, s32[512,2]{0,1:T(2,128)}, u32[]{:S(2)}) copy-start(s32[512,2]{0,1:T(2,128)} %param.22) | copy-start | bytes 12292
  0.7 14.0 %copy-start.14 = (s32[512]{0:T(512)S(1)}, s32[512]{0:T(512)}, u32[]{:S(2)}) copy-start(s32[512]{0:T(512)} %param.24) | copy-start | bytes 6148
  0.7 14.0 %copy-start.15 = (s32[512,1]{0,1:T(1,128)S(1)}, s32[512,1]{0,1:T(1,128)}, u32[]{:S(2)}) copy-start(s32[512,1]{0,1:T(1,128)} %param.23) | copy-start | bytes 6148
  3.2 20.9 %all-to-all-start = ((s32[128,1,128]{2,1,0:T(1,128)}), s32[128,1,128]{2,1,0:T(1,128)S(1)}, u32[]{:S(2)}, u32[]{:S(2)}) async-start(s32[128,1,128]{2,1,0:T(1,128)} %get-tuple-element.10), calls=%async_computation | async-start | bytes 131072 | tf_op jit(solution)/shard_map/all_to_all | solution.py:400
  14.8 1.9 %copy-start = (bf16[316,64,64]{0,2,1:T(8,128)(2,1)S(1)}, bf16[316,64,64]{0,2,1:T(8,128)(2,1)}, u32[]{:S(2)}) copy-start(bf16[316,64,64]{0,2,1:T(8,128)(2,1)} %param.18) | copy-start | bytes 7766020
  16.6 0.7 %copy-start.16 = (s32[1,2048]{1,0:T(1,128)S(1)}, s32[1,2048]{1,0:T(1,128)}, u32[]{:S(2)}) copy-start(s32[1,2048]{1,0:T(1,128)} %get-tuple-element.11.f_pos) | copy-start | bytes 24580
  17.3 0.7 %copy-start.18 = (s32[1,512]{1,0:T(1,128)S(1)}, s32[1,512]{1,0:T(1,128)}, u32[]{:S(2)}) copy-start(s32[1,512]{1,0:T(1,128)} %get-tuple-element.12.c_pos) | copy-start | bytes 6148
  26.2 7.2 %copy-start.4 = (s32[8192,2]{0,1:T(2,128)S(1)}, s32[8192,2]{0,1:T(2,128)}, u32[]{:S(2)}) copy-start(s32[8192,2]{0,1:T(2,128)} %param.25) | copy-start | bytes 196612
  26.2 7.3 %copy-start.5 = (s32[8192]{0:T(1024)S(1)}, s32[8192]{0:T(1024)}, u32[]{:S(2)}) copy-start(s32[8192]{0:T(1024)} %param.26) | copy-start | bytes 98308
  26.2 7.3 %copy-start.10 = (s32[1024,2]{0,1:T(2,128)S(1)}, s32[1024,2]{0,1:T(2,128)}, u32[]{:S(2)}) copy-start(s32[1024,2]{0,1:T(2,128)} %param.20) | copy-start | bytes 24580
  26.2 7.3 %copy-start.12 = (s32[1024]{0:T(1024)S(1)}, s32[1024]{0:T(1024)}, u32[]{:S(2)}) copy-start(s32[1024]{0:T(1024)} %param.21) | copy-start | bytes 12292
  26.2 29.4 %all-to-all-start.1 = ((bf16[128,40,128]{2,1,0:T(8,128)(2,1)}), bf16[128,40,128]{2,1,0:T(8,128)(2,1)S(1)}, u32[]{:S(2)}, u32[]{:S(2)}) async-start(bf16[128,40,128]{2,1,0:T(8,128)(2,1)} %shard_map.160), calls=%async_computation.1 | async-start | bytes 2621440 | tf_op jit(solution)/shard_map/all_to_all | solution.py:432
  33.4 1.9 %copy-start.1 = (bf16[316,64,64]{0,2,1:T(8,128)(2,1)S(1)}, bf16[316,64,64]{0,2,1:T(8,128)(2,1)}, u32[]{:S(2)}) copy-start(bf16[316,64,64]{0,2,1:T(8,128)(2,1)} %param.18) | copy-start | bytes 7766020
  35.3 20.2 %copy-start.2 = (bf16[8,64,64]{2,1,0:T(8,128)(2,1)S(1)}, bf16[8,64,64]{2,1,0:T(8,128)(2,1)}, u32[]{:S(2)}) copy-start(bf16[8,64,64]{2,1,0:T(8,128)(2,1)} %maps.1) | copy-start | bytes 196612
  35.3 20.2 %copy-start.6 = (f32[64,64]{1,0:T(8,128)S(1)}, f32[64,64]{1,0:T(8,128)}, u32[]{:S(2)}) copy-start(f32[64,64]{1,0:T(8,128)} %parent.1) | copy-start | bytes 49156
  35.3 20.2 %copy-start.17 = (s32[1,2048]{1,0:T(1,128)S(1)}, s32[1,2048]{1,0:T(1,128)}, u32[]{:S(2)}) copy-start(s32[1,2048]{1,0:T(1,128)} %get-tuple-element.11.f_pos) | copy-start | bytes 24580
  35.3 20.2 %copy-start.19 = (s32[1,512]{1,0:T(1,128)S(1)}, s32[1,512]{1,0:T(1,128)}, u32[]{:S(2)}) copy-start(s32[1,512]{1,0:T(1,128)} %get-tuple-element.12.c_pos) | copy-start | bytes 6148

commit v3 on v2

--- a/solution.py
+++ b/solution.py
@@ -24,7 +24,7 @@
 NEAR_GROUPS = G_NEAR_F + G_NEAR_C
 NEAR_BLOCK = 4096
 PM_ROWS = 512
-MIB_1, MIB_2, MIB_3, MIB_4, MIB_5 = 60, 32, 24, 40, 40
+MIB_1, MIB_2, MIB_3, MIB_4, MIB_5 = 16, 32, 24, 40, 40
 
 
 def mm(a, b):
@@ -79,22 +79,27 @@
     return jnp.where((down <= across) | (across >= 128), 1.0, 0.0).astype(BF16)
 
 
-def fetch(pairs, sems):
-    copies = [pltpu.make_async_copy(a, b, sems.at[i]) for i, (a, b) in enumerate(pairs)]
+def route_kernel(
+    f_owner_in, f_boxes_in, c_owner_in, c_boxes_in, ops_in,
+    slots_ref, f_pos, c_pos, f_owner, f_boxes, c_owner, c_boxes, ops,
+    sems,
+):
+    copies = [
+        pltpu.make_async_copy(source, target, sems.at[i])
+        for i, (source, target) in enumerate(
+            [
+                (f_owner_in, f_owner),
+                (c_owner_in, c_owner),
+                (f_boxes_in, f_boxes),
+                (c_boxes_in, c_boxes),
+                (ops_in, ops),
+            ]
+        )
+    ]
     for copy in copies:
         copy.start()
-    for copy in copies:
+    for copy in copies[:4]:
         copy.wait()
-
-
-def route_kernel(
-    f_owner_in, f_boxes_in, c_owner_in, c_boxes_in, slots_ref, f_pos, c_pos,
-    f_owner, f_boxes, c_owner, c_boxes, sems,
-):
-    fetch(
-        [(f_owner_in, f_owner), (f_boxes_in, f_boxes), (c_owner_in, c_owner), (c_boxes_in, c_boxes)],
-        sems,
-    )
     f_blocks, c_blocks = f_owner.shape[1] // 128, c_owner.shape[1] // 128
     hits = [
         lax.broadcasted_iota(I32, (DEV, 128), 0) == ref[:, b * 128:(b + 1) * 128]
@@ -134,6 +139,7 @@
     rest = jnp.zeros((128 - CAP_F - CAP_C, DEV), F32)
     table = jnp.concatenate([fine, coarse, rest], axis=0)
     slots_ref[:, 0, :] = jnp.transpose(table).astype(I32)
+    copies[4].wait()
 
 
 def pick_operators(ops, kinds, flat, out):
@@ -381,21 +387,27 @@
     ops = jnp.transpose(operators, (1, 2, 0))
 
     n_f, n_c = f_owner.shape[1], c_owner.shape[1]
-    slots, f_pos, c_pos = call(
+    slots, f_pos, c_pos, f_owner, f_far, c_owner, c_far, ops = call(
         route_kernel,
-        (sds((DEV, 1, 128), I32), sds((1, n_f), I32), sds((1, n_c), I32)),
-        [
+        (
+            sds((DEV, 1, 128), I32),
+            pltpu.VMEM((1, n_f), I32),
+            pltpu.VMEM((1, n_c), I32),
             pltpu.VMEM((1, n_f), I32),
             pltpu.VMEM((2, n_f), I32),
             pltpu.VMEM((1, n_c), I32),
             pltpu.VMEM((2, n_c), I32),
-            pltpu.SemaphoreType.DMA((4,)),
-        ],
+            pltpu.VMEM(ops.shape, BF16),
+        ),
+        [pltpu.SemaphoreType.DMA((5,))],
         MIB_1,
         10**9,
         10**6,
-        f_owner, f_far, c_owner, c_far,
-        in_specs=[pl.BlockSpec(memory_space=pltpu.HBM)] * 4,
+        *[
+            pltpu.with_memory_space_constraint(x, pltpu.HBM)
+            for x in (f_owner, f_far, c_owner, c_far, ops)
+        ],
+        in_specs=[pl.BlockSpec(memory_space=pltpu.HBM)] * 5,
     )
     asked = lax.all_to_all(slots, ("oct", "box"), split_axis=0, concat_axis=0, tiled=True)
     sel, f_part, c_part = call(
@@ -422,7 +434,7 @@
     )
     sent = call(
         reply_kernel,
-        sds((DEV, ROWS, 128), BF16),
+        pltpu.VMEM((DEV, ROWS, 128), BF16),
         [pltpu.VMEM((DEV * ROWS_F, 128), F32), pltpu.VMEM((DEV * 2 * ROWS_C, 128), F32)],
         MIB_3,
         10**9,

time: 60 us -> 60.3 us (level)
  waiting for transfers between devices: 14.1 us -> 15.5 us
  starting transfers between devices: 18.7 us -> 17.3 us
    all_to_all x1, waiting for transfers between devices: 2.56 us -> 3.97 us  [on_device(): lax.all_to_all(slots, ('oct', 'box'), split_axis=0, concat_axis=0, tiled=...]
    all_to_all x1, starting transfers between devices: 7.22 us -> 5.85 us  [on_device(): lax.all_to_all(sent, ('oct', 'box'), split_axis=0, concat_axis=0, tiled=T...]
    unnamed x40 -> x26, local copies, waits for them, and re-layouts: 5.2 us -> 5.44 us
where the time goes in v3:
time: 60.3 us; the launch traced here: 60 us
  Pallas kernels  20.8 us (34%)
  starting transfers between devices  17.3 us (29%)
  waiting for transfers between devices  15.5 us (26%)
  local copies, waits for them, and re-layouts  5.44 us (9%)
  between operations  0.79 us (1%)
    pallas_call x5, Pallas kernels, call(): pl.pallas_call(kernel, out_shape=out_shape, scratch_shapes=scratch, compi...  20.8 us
    all_to_all x1, waiting for transfers between devices, on_device(): lax.all_to_all(sent, ('oct', 'box'), split_axis=0, concat_axis=0, tiled=T...  11.6 us
    all_to_all x1, starting transfers between devices, on_device(): lax.all_to_all(slots, ('oct', 'box'), split_axis=0, concat_axis=0, tiled=...  11.5 us
    all_to_all x1, starting transfers between devices, on_device(): lax.all_to_all(sent, ('oct', 'box'), split_axis=0, concat_axis=0, tiled=T...  5.85 us
    unnamed x26, local copies, waits for them, and re-layouts  5.44 us
    all_to_all x1, waiting for transfers between devices, on_device(): lax.all_to_all(slots, ('oct', 'box'), split_axis=0, concat_axis=0, tiled=...  3.97 us
  transfers between devices with their start and end apart: 2, of which 2 were waited for; matrix products, arithmetic and copies ran while one was open for 0% of the time, Pallas kernels for 20%

profile of v3, /device:TPU:1, one launch (start us, length us, event | category | flops | bytes accessed | tf_op | source)
XLA Modules:
  0.0 60.0 jit_solution(11150022255477117478)
XLA Ops:
  0.6 0.0 copy-start.1
  0.6 0.0 copy-start.5
  0.7 0.0 copy-start.6
  0.7 0.0 copy-start.9
  0.7 2.7 %shard_map.158 = (s32[128,1,128]{2,1,0:T(1,128)}, s32[1,2048]{1,0:T(1,128)S(1)}, s32[1,512]{1,0:T(1,128)S(1)}, s32[1,2048]{1,0:T(1,128)S(1)}, s32[2,2048]{1,0:T(...) custom-call(s32[1,2048]{1,0:T(1,128)} %bitcast.19, s32[2,2048]{1,0:T(2,128)} %bitcast.18, ...), custom_call_target="tpu_custom_call" | custom-call | flops 1000000000 | bytes 1000000 | tf_op jit(solution)/shard_map/pallas_call | solution.py:354
  3.3 0.0 copy-start.10
  3.4 1.6 %copy-done.10 = bf16[64,64,316]{2,1,0:T(8,128)(2,1)} copy-done((bf16[64,64,316]{2,1,0:T(8,128)(2,1)}, bf16[64,64,316]{2,1,0:T(8,128)(2,1)S(1)}, u32[]{:S(2)}) %copy-start.10) | copy-done | bytes 2588696
  5.0 11.5 %all-to-all-start = ((s32[128,1,128]{2,1,0:T(1,128)}), s32[128,1,128]{2,1,0:T(1,128)S(1)}, u32[]{:S(2)}, u32[]{:S(2)}) async-start(s32[128,1,128]{2,1,0:T(1,128)} %get-tuple-element.15), calls=%async_computation | async-start | bytes 131072 | tf_op jit(solution)/shard_map/all_to_all | solution.py:412
  16.5 0.0 copy-done.1
  16.5 0.0 copy-done.5
  16.5 0.0 copy-done.6
  16.5 0.0 copy-done.9
  16.5 0.0 copy-start.11
  16.5 1.9 %copy-done.11 = bf16[64,64,316]{2,1,0:T(8,128)(2,1)S(1)} copy-done((bf16[64,64,316]{2,1,0:T(8,128)(2,1)S(1)}, bf16[64,64,316]{2,1,0:T(8,128)(2,1)}, u32[]{:S(2)}) %copy-start.11) | copy-done | bytes 2588696
  18.4 3.5 %shard_map.159 = (bf16[24,64,64]{2,1,0:T(8,128)(2,1)S(1)}, bf16[128,16,128]{2,1,0:T(8,128)(2,1)S(1)}, f32[4,128,128]{2,1,0:T(8,128)S(1)}) custom-call(bf16[64,64,316]{2,1,0:T(8,128)(2,1)S(1)} %copy-done.11, s32[16,128]{1,0:T(8,128)S(1)} %bitcast.13, s32[4,128]{1,0:T(4,128)S(1)} %bitcast.16, bf16[64,512]{1,0:T(8,128)(2,1)S(1)} %copy-done.1, ...), custom_call_target="tpu_custom_call" | custom-call | flops 5000000000 | bytes 10000000 | tf_op jit(solution)/shard_map/pallas_call | solution.py:354
  21.9 4.0 %all-to-all-done.slots = s32[128,1,128]{2,1,0:T(1,128)S(1)} async-done(((s32[128,1,128]{2,1,0:T(1,128)}), s32[128,1,128]{2,1,0:T(1,128)S(1)}, u32[]{:S(2)}, u32[]{:S(2)}) %all-to-all-start) | async-done | bytes 65568 | tf_op jit(solution)/shard_map/all_to_all | solution.py:412
  25.9 0.0 copy-start.2
  25.9 0.0 copy-start.3
  25.9 0.0 copy-start.7
  25.9 0.0 copy-start.8
  25.9 2.0 %shard_map.160 = bf16[128,40,128]{2,1,0:T(8,128)(2,1)} custom-call(s32[128,1,128]{2,1,0:T(1,128)S(1)} %all-to-all-done.slots, bf16[64,512]{1,0:T(8,128)(2,1)S(1)} %copy-done.1, bf16[64,64]{1,0:T(8,128)(2,1)S(1)} %copy-done.5, bf16[128,16,128]{2,1,0:T(8,128)(2,1)S(1)} %get-tuple-element.23.f_part, f32[4,128,128]{2,1,0:T(8,128)S(1)} %get-tuple-element.24.c_part), custom_call_target="tpu_custom_call" | custom-call | flops 1000000000 | bytes 1000000 | tf_op jit(solution)/shard_map/pallas_call | solution.py:354
  28.0 5.9 %all-to-all-start.1 = ((bf16[128,40,128]{2,1,0:T(8,128)(2,1)}), bf16[128,40,128]{2,1,0:T(8,128)(2,1)S(1)}, u32[]{:S(2)}, u32[]{:S(2)}) async-start(bf16[128,40,128]{2,1,0:T(8,128)(2,1)} %shard_map.160), calls=%async_computation.1 | async-start | bytes 2621440 | tf_op jit(solution)/shard_map/all_to_all | solution.py:444
  33.8 0.0 copy-done.2
  33.8 0.0 copy-done.3
  33.8 0.0 copy-done.7
  33.9 0.0 copy-done.8
  33.9 0.0 copy-start.12
  33.9 1.9 %copy-done.12 = bf16[64,64,316]{2,1,0:T(8,128)(2,1)S(1)} copy-done((bf16[64,64,316]{2,1,0:T(8,128)(2,1)S(1)}, bf16[64,64,316]{2,1,0:T(8,128)(2,1)}, u32[]{:S(2)}) %copy-start.12) | copy-done | bytes 2588696
  35.8 0.0 copy-start
  35.8 0.0 copy-start.4
  35.8 8.6 %shard_map.161 = (f32[128,256]{1,0:T(8,128)S(1)}, f32[64,64]{1,0:T(8,128)S(1)}) custom-call(bf16[64,64,316]{2,1,0:T(8,128)(2,1)S(1)} %copy-done.12, s32[64,128]{1,0:T(8,128)S(1)} %bitcast.12, s32[8,128]{1,0:T(8,128)S(1)} %bitcast.15, bf16[64,512]{1,0:T(8,128)(2,1)S(1)} %copy-done.1, bf16[64,64]{1,0:T(8,128)(2,1)S(1)} %copy-done.5, s32[2,8192]{1,0:T(2,128)S(1)} %bitcast.11, ...), custom_call_target="tpu_custom_call" | custom-call | flops 10000000000 | bytes 10000000 | tf_op jit(solution)/shard_map/pallas_call | solution.py:354
  44.4 11.6 %all-to-all-done.1.got = bf16[128,40,128]{2,1,0:T(8,128)(2,1)S(1)} async-done(((bf16[128,40,128]{2,1,0:T(8,128)(2,1)}), bf16[128,40,128]{2,1,0:T(8,128)(2,1)S(1)}, u32[]{:S(2)}, u32[]{:S(2)}) %all-to-all-start.1) | async-done | bytes 1310752 | tf_op jit(solution)/shard_map/all_to_all | solution.py:444
  56.0 0.0 copy-done
  56.0 0.0 copy-done.4
  56.0 4.0 %shard_map.162 = (bf16[64,64]{1,0:T(8,128)(2,1)}, bf16[64,512]{1,0:T(8,128)(2,1)}) custom-call(bf16[128,40,128]{2,1,0:T(8,128)(2,1)S(1)} %all-to-all-done.1.got, s32[128,1,128]{2,1,0:T(1,128)S(1)} %all-to-all-done.slots, bf16[24,64,64]{2,1,0:T(8,128)(2,1)S(1)} %get-tuple-element.25.sel, f32[128,256]{1,0:T(8,128)S(1)} %get-tuple-element.26.f_near, ...), custom_call_target="tpu_custom_call" | custom-call | flops 3000000000 | bytes 10000000 | tf_op jit(solution)/shard_map/pallas_call | solution.py:354
Async XLA Ops:
  0.6 15.9 %copy-start.1 = (bf16[64,512]{1,0:T(8,128)(2,1)S(1)}, bf16[64,512]{1,0:T(8,128)(2,1)}, u32[]{:S(2)}) copy-start(bf16[64,512]{1,0:T(8,128)(2,1)} %fm.5) | copy-start | bytes 196612
  0.6 15.9 %copy-start.5 = (bf16[64,64]{1,0:T(8,128)(2,1)S(1)}, bf16[64,64]{1,0:T(8,128)(2,1)}, u32[]{:S(2)}) copy-start(bf16[64,64]{1,0:T(8,128)(2,1)} %cm.5) | copy-start | bytes 24580
  0.7 15.9 %copy-start.6 = (s32[2048]{0:T(1024)S(1)}, s32[2048]{0:T(1024)}, u32[]{:S(2)}) copy-start(s32[2048]{0:T(1024)} %param.29) | copy-start | bytes 24580
  0.7 15.9 %copy-start.9 = (s32[512]{0:T(512)S(1)}, s32[512]{0:T(512)}, u32[]{:S(2)}) copy-start(s32[512]{0:T(512)} %param.24) | copy-start | bytes 6148
  3.3 1.6 %copy-start.10 = (bf16[64,64,316]{2,1,0:T(8,128)(2,1)}, bf16[64,64,316]{2,1,0:T(8,128)(2,1)S(1)}, u32[]{:S(2)}) copy-start(bf16[64,64,316]{2,1,0:T(8,128)(2,1)S(1)} %get-tuple-element.16.ops) | copy-start | bytes 7766020
  5.0 20.9 %all-to-all-start = ((s32[128,1,128]{2,1,0:T(1,128)}), s32[128,1,128]{2,1,0:T(1,128)S(1)}, u32[]{:S(2)}, u32[]{:S(2)}) async-start(s32[128,1,128]{2,1,0:T(1,128)} %get-tuple-element.15), calls=%async_computation | async-start | bytes 131072 | tf_op jit(solution)/shard_map/all_to_all | solution.py:412
  16.5 1.9 %copy-start.11 = (bf16[64,64,316]{2,1,0:T(8,128)(2,1)S(1)}, bf16[64,64,316]{2,1,0:T(8,128)(2,1)}, u32[]{:S(2)}) copy-start(bf16[64,64,316]{2,1,0:T(8,128)(2,1)} %copy-done.10) | copy-start | bytes 7766020
  25.9 7.9 %copy-start.2 = (s32[8192,2]{0,1:T(2,128)S(1)}, s32[8192,2]{0,1:T(2,128)}, u32[]{:S(2)}) copy-start(s32[8192,2]{0,1:T(2,128)} %param.25) | copy-start | bytes 196612
  25.9 7.9 %copy-start.3 = (s32[8192]{0:T(1024)S(1)}, s32[8192]{0:T(1024)}, u32[]{:S(2)}) copy-start(s32[8192]{0:T(1024)} %param.26) | copy-start | bytes 98308
  25.9 7.9 %copy-start.7 = (s32[1024,2]{0,1:T(2,128)S(1)}, s32[1024,2]{0,1:T(2,128)}, u32[]{:S(2)}) copy-start(s32[1024,2]{0,1:T(2,128)} %param.20) | copy-start | bytes 24580
  25.9 7.9 %copy-start.8 = (s32[1024]{0:T(1024)S(1)}, s32[1024]{0:T(1024)}, u32[]{:S(2)}) copy-start(s32[1024]{0:T(1024)} %param.21) | copy-start | bytes 12292
  28.0 28.0 %all-to-all-start.1 = ((bf16[128,40,128]{2,1,0:T(8,128)(2,1)}), bf16[128,40,128]{2,1,0:T(8,128)(2,1)S(1)}, u32[]{:S(2)}, u32[]{:S(2)}) async-start(bf16[128,40,128]{2,1,0:T(8,128)(2,1)} %shard_map.160), calls=%async_computation.1 | async-start | bytes 2621440 | tf_op jit(solution)/shard_map/all_to_all | solution.py:444
  33.9 1.9 %copy-start.12 = (bf16[64,64,316]{2,1,0:T(8,128)(2,1)S(1)}, bf16[64,64,316]{2,1,0:T(8,128)(2,1)}, u32[]{:S(2)}) copy-start(bf16[64,64,316]{2,1,0:T(8,128)(2,1)} %copy-done.10) | copy-start | bytes 7766020
  35.8 20.2 %copy-start = (bf16[8,64,64]{2,1,0:T(8,128)(2,1)S(1)}, bf16[8,64,64]{2,1,0:T(8,128)(2,1)}, u32[]{:S(2)}) copy-start(bf16[8,64,64]{2,1,0:T(8,128)(2,1)} %maps.1) | copy-start | bytes 196612
  35.8 20.2 %copy-start.4 = (f32[64,64]{1,0:T(8,128)S(1)}, f32[64,64]{1,0:T(8,128)}, u32[]{:S(2)}) copy-start(f32[64,64]{1,0:T(8,128)} %parent.1) | copy-start | bytes 49156

commit v4 on v3

--- a/solution.py
+++ b/solution.py
@@ -24,7 +24,8 @@
 NEAR_GROUPS = G_NEAR_F + G_NEAR_C
 NEAR_BLOCK = 4096
 PM_ROWS = 512
-MIB_1, MIB_2, MIB_3, MIB_4, MIB_5 = 16, 32, 24, 40, 40
+OPS_CHUNKS = 2
+MIB_1, MIB_2, MIB_3, MIB_4, MIB_5 = 16, 36, 24, 44, 40
 
 
 def mm(a, b):
@@ -80,9 +81,8 @@
 
 
 def route_kernel(
-    f_owner_in, f_boxes_in, c_owner_in, c_boxes_in, ops_in,
-    slots_ref, f_pos, c_pos, f_owner, f_boxes, c_owner, c_boxes, ops,
-    sems,
+    f_owner_in, f_boxes_in, c_owner_in, c_boxes_in,
+    slots_ref, f_pos, c_pos, f_owner, f_boxes, c_owner, c_boxes, sems,
 ):
     copies = [
         pltpu.make_async_copy(source, target, sems.at[i])
@@ -92,13 +92,12 @@
                 (c_owner_in, c_owner),
                 (f_boxes_in, f_boxes),
                 (c_boxes_in, c_boxes),
-                (ops_in, ops),
             ]
         )
     ]
     for copy in copies:
         copy.start()
-    for copy in copies[:4]:
+    for copy in copies:
         copy.wait()
     f_blocks, c_blocks = f_owner.shape[1] // 128, c_owner.shape[1] // 128
     hits = [
@@ -139,14 +138,25 @@
     rest = jnp.zeros((128 - CAP_F - CAP_C, DEV), F32)
     table = jnp.concatenate([fine, coarse, rest], axis=0)
     slots_ref[:, 0, :] = jnp.transpose(table).astype(I32)
-    copies[4].wait()
-
-
-def pick_operators(ops, kinds, flat, out):
+
+
+def operator_copies(ops_in, ops, sems):
+    each = RANK // OPS_CHUNKS
+    return [
+        pltpu.make_async_copy(
+            ops_in.at[pl.ds(k * each, each)], ops.at[pl.ds(k * each, each)], sems.at[k]
+        )
+        for k in range(OPS_CHUNKS)
+    ]
+
+
+def pick_operators(copies, ops, kinds, flat, out):
     groups, nt = kinds.shape[0], ops.shape[2]
     hot = jnp.where(kinds[:, 0:1] == lax.broadcasted_iota(I32, (groups, nt), 1), 1.0, 0.0)
     hot = hot.astype(BF16)
     for quad in range(RANK // 4):
+        if quad % (RANK // 4 // OPS_CHUNKS) == 0:
+            copies[quad // (RANK // 4 // OPS_CHUNKS)].wait()
         rows = ops[quad * 4:(quad + 1) * 4].reshape(256, nt)
         got = mm_nt(hot, rows)
         for k in range(4):
@@ -155,42 +165,39 @@
 
 
 def outgoing_kernel(
-    ops, s_ff, s_fc, fm, cm, f_owner, f_boxes, f_pos, c_owner, c_boxes, c_pos,
-    sel_ref, f_part, c_part, kinds, kf, pm, hot_out, flat,
+    ops_in, s_ff, s_fc, fm, cm, f_owner, f_boxes, f_pos, c_owner, c_boxes, c_pos,
+    sel_ref, f_part, c_part, ops, f_vec, c_vec, kinds, kf, pm, hot_out, flat, sems,
 ):
+    copies = operator_copies(ops_in, ops, sems)
+    for copy in copies:
+        copy.start()
+    row = f_boxes[0:1, :]
+    f_vec[...] = pick_fine(half_stack(fm[...]), one_hot(row & 255, 256), row).astype(BF16)
+    c_vec[...] = mm(cm[...], one_hot(c_boxes[0:1, :], 64)).astype(BF16)
+    pos = f_pos[...]
+    hot_out[...] = one_hot((pos >> 4) * DEV + f_owner[...], 2 * DEV)
     kinds[...] = jnp.zeros_like(kinds)
     kinds[0:G_FAR_F] = s_ff[...]
     kinds[G_FAR_F:G_FAR_F + G_FAR_C] = s_fc[...]
-    pick_operators(ops, kinds, kf, sel_ref)
-
-    row = c_boxes[0:1, :]
-    vec = mm(cm[...], one_hot(row, 64)).astype(BF16)
+    pick_operators(copies, ops, kinds, kf, sel_ref)
+
     part = jnp.concatenate(
         [
-            mm_tn(sel_ref[G_FAR_F + g], vec[:, g * 128:(g + 1) * 128])
+            mm_tn(sel_ref[G_FAR_F + g], c_vec[:, g * 128:(g + 1) * 128])
             for g in range(G_FAR_C)
         ],
         axis=1,
     )
-    pos = c_pos[...]
-    pieces = [jnp.where(pos == k, part, 0.0).astype(BF16) for k in range(CAP_C)]
+    at = c_pos[...]
+    pieces = [jnp.where(at == k, part, 0.0).astype(BF16) for k in range(CAP_C)]
     big = mm_nt(jnp.concatenate(pieces, axis=0), one_hot(c_owner[...], DEV))
     for kp in range(ROWS_C):
         c_part[kp] = jnp.transpose(big[kp * 128:(kp + 1) * 128])
 
-    stack = half_stack(fm[...])
-    row = f_boxes[0:1, :]
-    vec = pick_fine(stack, one_hot(row & 255, 256), row).astype(BF16)
     part = jnp.concatenate(
-        [
-            mm_tn(sel_ref[g], vec[:, g * 128:(g + 1) * 128])
-            for g in range(G_FAR_F)
-        ],
-        axis=1,
+        [mm_tn(sel_ref[g], f_vec[:, g * 128:(g + 1) * 128]) for g in range(G_FAR_F)], axis=1
     )
     part = (2.0 * part).astype(BF16)
-    pos = f_pos[...]
-    hot_out[...] = one_hot((pos >> 4) * DEV + f_owner[...], 2 * DEV)
     step = jnp.broadcast_to((pos & (HALF_CAP - 1)).astype(BF16), part.shape)
     none = jnp.zeros((), BF16)
     for k in range(HALF_CAP):
@@ -238,10 +245,15 @@
     )
 
 
-def near_kernel(ops, s_nf, s_nc, fm, cm, f_boxes, c_boxes, f_out, c_out, kinds, kf, sel, f_sum):
+def near_kernel(
+    ops_in, s_nf, s_nc, fm, cm, f_boxes, c_boxes, f_out, c_out, ops, kinds, kf, sel, f_sum, sems
+):
+    copies = operator_copies(ops_in, ops, sems)
+    for copy in copies:
+        copy.start()
     kinds[0:G_NEAR_F] = s_nf[...]
     kinds[G_NEAR_F:NEAR_GROUPS] = s_nc[...]
-    pick_operators(ops, kinds, kf, sel)
+    pick_operators(copies, ops, kinds, kf, sel)
     stack = half_stack(fm[...])
     f_sum[...] = jnp.zeros_like(f_sum)
 
@@ -381,13 +393,18 @@
     def sds(shape, dtype):
         return jax.ShapeDtypeStruct(shape, dtype)
 
+    def in_hbm(x):
+        return pltpu.with_memory_space_constraint(x, pltpu.HBM)
+
     fm, cm = fine_multipole, coarse_multipole
+    vmem = pl.BlockSpec(memory_space=pltpu.VMEM)
+    hbm = pl.BlockSpec(memory_space=pltpu.HBM)
     f_owner, c_owner = fine_far_owner.T, coarse_far_owner.T
     f_far, c_far = fine_far_boxes.T, coarse_far_boxes.T
-    ops = jnp.transpose(operators, (1, 2, 0))
+    ops = in_hbm(jnp.transpose(operators, (1, 2, 0)))
 
     n_f, n_c = f_owner.shape[1], c_owner.shape[1]
-    slots, f_pos, c_pos, f_owner, f_far, c_owner, c_far, ops = call(
+    slots, f_pos, c_pos, f_owner, f_far, c_owner, c_far = call(
         route_kernel,
         (
             sds((DEV, 1, 128), I32),
@@ -397,17 +414,13 @@
             pltpu.VMEM((2, n_f), I32),
             pltpu.VMEM((1, n_c), I32),
             pltpu.VMEM((2, n_c), I32),
-            pltpu.VMEM(ops.shape, BF16),
         ),
-        [pltpu.SemaphoreType.DMA((5,))],
+        [pltpu.SemaphoreType.DMA((4,))],
         MIB_1,
         10**9,
         10**6,
-        *[
-            pltpu.with_memory_space_constraint(x, pltpu.HBM)
-            for x in (f_owner, f_far, c_owner, c_far, ops)
-        ],
-        in_specs=[pl.BlockSpec(memory_space=pltpu.HBM)] * 5,
+        *[in_hbm(x) for x in (f_owner, f_far, c_owner, c_far)],
+        in_specs=[hbm] * 4,
     )
     asked = lax.all_to_all(slots, ("oct", "box"), split_axis=0, concat_axis=0, tiled=True)
     sel, f_part, c_part = call(
@@ -418,11 +431,15 @@
             sds((ROWS_C, DEV, 128), F32),
         ),
         [
+            pltpu.VMEM(ops.shape, BF16),
+            pltpu.VMEM((RANK, n_f), BF16),
+            pltpu.VMEM((RANK, n_c), BF16),
             pltpu.VMEM((FAR_GROUPS, 128), I32),
             pltpu.VMEM((FAR_GROUPS * RANK, RANK), F32),
             pltpu.VMEM((HALF_CAP * RANK, n_f), BF16),
             pltpu.VMEM((2 * DEV, n_f), BF16),
             pltpu.VMEM((DEV * ROWS_F, 128), F32),
+            pltpu.SemaphoreType.DMA((OPS_CHUNKS,)),
         ],
         MIB_2,
         5 * 10**9,
@@ -431,10 +448,11 @@
         fine_far_shift.reshape(-1, 128),
         coarse_far_shift.reshape(-1, 128),
         fm, cm, f_owner, f_far, f_pos, c_owner, c_far, c_pos,
+        in_specs=[hbm] + [vmem] * 10,
     )
     sent = call(
         reply_kernel,
-        pltpu.VMEM((DEV, ROWS, 128), BF16),
+        sds((DEV, ROWS, 128), BF16),
         [pltpu.VMEM((DEV * ROWS_F, 128), F32), pltpu.VMEM((DEV * 2 * ROWS_C, 128), F32)],
         MIB_3,
         10**9,
@@ -446,10 +464,12 @@
         near_kernel,
         (sds((2 * RANK, 256), F32), sds((RANK, 64), F32)),
         [
+            pltpu.VMEM(ops.shape, BF16),
             pltpu.VMEM((NEAR_GROUPS, 128), I32),
             pltpu.VMEM((NEAR_GROUPS * RANK, RANK), F32),
             pltpu.VMEM((NEAR_GROUPS, RANK, RANK), BF16),
             pltpu.VMEM((4 * RANK, 256), F32),
+            pltpu.SemaphoreType.DMA((OPS_CHUNKS,)),
         ],
         MIB_4,
         10**10,
@@ -458,6 +478,7 @@
         fine_near_shift.reshape(-1, 128),
         coarse_near_shift.reshape(-1, 128),
         fm, cm, fine_near_boxes.T, coarse_near_boxes.T,
+        in_specs=[hbm] + [vmem] * 6,
     )
     return call(
         final_kernel,

time: 60.3 us -> 58.2 us (0.965)
  local copies, waits for them, and re-layouts: 5.44 us -> 0.04 us
  Pallas kernels: 20.8 us -> 23.9 us
    unnamed x26 -> x20, local copies, waits for them, and re-layouts: 5.44 us -> 0.04 us
    pallas_call x5, Pallas kernels: 20.8 us -> 23.9 us  [call(): pl.pallas_call(kernel, out_shape=out_shape, scratch_shapes=scratch, compi...]
  transfers between devices with their start and end apart: 2 -> 2, of which waited for: 2 -> 2; matrix products, arithmetic and copies ran while one was open for 0% -> 0% of each run, Pallas kernels for 20% -> 27%
where the time goes in v4:
time: 58.2 us; the launch traced here: 57.9 us
  Pallas kernels  23.9 us (41%)
  starting transfers between devices  17.1 us (29%)
  waiting for transfers between devices  16 us (27%)
  between operations  0.79 us (1%)
    pallas_call x5, Pallas kernels, call(): pl.pallas_call(kernel, out_shape=out_shape, scratch_shapes=scratch, compi...  23.9 us
    all_to_all x1, waiting for transfers between devices, on_device(): lax.all_to_all(sent, ('oct', 'box'), split_axis=0, concat_axis=0, tiled=T...  11.8 us
    all_to_all x1, starting transfers between devices, on_device(): lax.all_to_all(slots, ('oct', 'box'), split_axis=0, concat_axis=0, tiled=...  11.5 us
    all_to_all x1, starting transfers between devices, on_device(): lax.all_to_all(sent, ('oct', 'box'), split_axis=0, concat_axis=0, tiled=T...  5.65 us
    all_to_all x1, waiting for transfers between devices, on_device(): lax.all_to_all(slots, ('oct', 'box'), split_axis=0, concat_axis=0, tiled=...  4.14 us
  transfers between devices with their start and end apart: 2, of which 2 were waited for; matrix products, arithmetic and copies ran while one was open for 0% of the time, Pallas kernels for 27%

profile of v4, /device:TPU:1, one launch (start us, length us, event | category | flops | bytes accessed | tf_op | source)
XLA Modules:
  0.0 57.9 jit_solution(16039962339303111473)
XLA Ops:
  0.6 0.0 copy-start.1
  0.6 0.0 copy-start.5
  0.7 0.0 copy-start.6
  0.7 0.0 copy-start.9
  0.7 2.4 %shard_map.158 = (s32[128,1,128]{2,1,0:T(1,128)}, s32[1,2048]{1,0:T(1,128)S(1)}, s32[1,512]{1,0:T(1,128)S(1)}, s32[1,2048]{1,0:T(1,128)S(1)}, s32[2,2048]{1,0:T(...) custom-call(s32[1,2048]{1,0:T(1,128)} %bitcast.20, s32[2,2048]{1,0:T(2,128)} %bitcast.19, s32[1,512]{1,0:T(1,128)} %bitcast.22, ...), custom_call_target="tpu_custom_call" | custom-call | flops 1000000000 | bytes 1000000 | tf_op jit(solution)/shard_map/pallas_call | solution.py:366
  3.1 11.5 %all-to-all-start = ((s32[128,1,128]{2,1,0:T(1,128)}), s32[128,1,128]{2,1,0:T(1,128)S(1)}, u32[]{:S(2)}, u32[]{:S(2)}) async-start(s32[128,1,128]{2,1,0:T(1,128)} %get-tuple-element.14), calls=%async_computation | async-start | bytes 131072 | tf_op jit(solution)/shard_map/all_to_all | solution.py:425
  14.6 0.0 copy-done.1
  14.6 0.0 copy-done.5
  14.6 0.0 copy-done.6
  14.7 0.0 copy-done.9
  14.7 5.2 %shard_map.159 = (bf16[24,64,64]{2,1,0:T(8,128)(2,1)S(1)}, bf16[128,16,128]{2,1,0:T(8,128)(2,1)S(1)}, f32[4,128,128]{2,1,0:T(8,128)S(1)}) custom-call(bf16[64,64,316]{2,1,0:T(8,128)(2,1)} %bitcast.17, s32[16,128]{1,0:T(8,128)S(1)} %bitcast.13, s32[4,128]{1,0:T(4,128)S(1)} %bitcast.16, bf16[64,512]{1,0:T(8,128)(2,1)S(1)} %copy-done.1, ...), custom_call_target="tpu_custom_call" | custom-call | flops 5000000000 | bytes 10000000 | tf_op jit(solution)/shard_map/pallas_call | solution.py:366
  19.9 4.1 %all-to-all-done.slots = s32[128,1,128]{2,1,0:T(1,128)S(1)} async-done(((s32[128,1,128]{2,1,0:T(1,128)}), s32[128,1,128]{2,1,0:T(1,128)S(1)}, u32[]{:S(2)}, u32[]{:S(2)}) %all-to-all-start) | async-done | bytes 65568 | tf_op jit(solution)/shard_map/all_to_all | solution.py:425
  24.0 2.0 %shard_map.160 = bf16[128,40,128]{2,1,0:T(8,128)(2,1)} custom-call(s32[128,1,128]{2,1,0:T(1,128)S(1)} %all-to-all-done.slots, bf16[64,512]{1,0:T(8,128)(2,1)S(1)} %copy-done.1, bf16[64,64]{1,0:T(8,128)(2,1)S(1)} %copy-done.5, bf16[128,16,128]{2,1,0:T(8,128)(2,1)S(1)} %get-tuple-element.21.f_part, f32[4,128,128]{2,1,0:T(8,128)S(1)} %get-tuple-element.22.c_part), custom_call_target="tpu_custom_call" | custom-call | flops 1000000000 | bytes 1000000 | tf_op jit(solution)/shard_map/pallas_call | solution.py:366
  26.1 0.0 copy-start.2
  26.1 0.0 copy-start.3
  26.1 0.0 copy-start.7
  26.1 0.0 copy-start.8
  26.1 5.6 %all-to-all-start.1 = ((bf16[128,40,128]{2,1,0:T(8,128)(2,1)}), bf16[128,40,128]{2,1,0:T(8,128)(2,1)S(1)}, u32[]{:S(2)}, u32[]{:S(2)}) async-start(bf16[128,40,128]{2,1,0:T(8,128)(2,1)} %shard_map.160), calls=%async_computation.1 | async-start | bytes 2621440 | tf_op jit(solution)/shard_map/all_to_all | solution.py:462
  31.7 0.0 copy-done.2
  31.8 0.0 copy-done.3
  31.8 0.0 copy-done.7
  31.8 0.0 copy-done.8
  31.8 0.0 copy-start
  31.8 0.0 copy-start.4
  31.8 10.3 %shard_map.161 = (f32[128,256]{1,0:T(8,128)S(1)}, f32[64,64]{1,0:T(8,128)S(1)}) custom-call(bf16[64,64,316]{2,1,0:T(8,128)(2,1)} %bitcast.18, s32[64,128]{1,0:T(8,128)S(1)} %bitcast.12, s32[8,128]{1,0:T(8,128)S(1)} %bitcast.15, bf16[64,512]{1,0:T(8,128)(2,1)S(1)} %copy-done.1, bf16[64,64]{1,0:T(8,128)(2,1)S(1)} %copy-done.5, s32[2,8192]{1,0:T(2,128)S(1)} %bitcast.11, ...), custom_call_target="tpu_custom_call" | custom-call | flops 10000000000 | bytes 10000000 | tf_op jit(solution)/shard_map/pallas_call | solution.py:366
  42.1 11.8 %all-to-all-done.1.got = bf16[128,40,128]{2,1,0:T(8,128)(2,1)S(1)} async-done(((bf16[128,40,128]{2,1,0:T(8,128)(2,1)}), bf16[128,40,128]{2,1,0:T(8,128)(2,1)S(1)}, u32[]{:S(2)}, u32[]{:S(2)}) %all-to-all-start.1) | async-done | bytes 1310752 | tf_op jit(solution)/shard_map/all_to_all | solution.py:462
  53.9 0.0 copy-done
  53.9 0.0 copy-done.4
  53.9 4.0 %shard_map.162 = (bf16[64,64]{1,0:T(8,128)(2,1)}, bf16[64,512]{1,0:T(8,128)(2,1)}) custom-call(bf16[128,40,128]{2,1,0:T(8,128)(2,1)S(1)} %all-to-all-done.1.got, s32[128,1,128]{2,1,0:T(1,128)S(1)} %all-to-all-done.slots, bf16[24,64,64]{2,1,0:T(8,128)(2,1)S(1)} %get-tuple-element.23.sel, f32[128,256]{1,0:T(8,128)S(1)} %get-tuple-element.24.f_near, ...), custom_call_target="tpu_custom_call" | custom-call | flops 3000000000 | bytes 10000000 | tf_op jit(solution)/shard_map/pallas_call | solution.py:366
Async XLA Ops:
  0.6 14.0 %copy-start.1 = (bf16[64,512]{1,0:T(8,128)(2,1)S(1)}, bf16[64,512]{1,0:T(8,128)(2,1)}, u32[]{:S(2)}) copy-start(bf16[64,512]{1,0:T(8,128)(2,1)} %fm.5) | copy-start | bytes 196612
  0.6 14.0 %copy-start.5 = (bf16[64,64]{1,0:T(8,128)(2,1)S(1)}, bf16[64,64]{1,0:T(8,128)(2,1)}, u32[]{:S(2)}) copy-start(bf16[64,64]{1,0:T(8,128)(2,1)} %cm.5) | copy-start | bytes 24580
  0.7 14.0 %copy-start.6 = (s32[2048]{0:T(1024)S(1)}, s32[2048]{0:T(1024)}, u32[]{:S(2)}) copy-start(s32[2048]{0:T(1024)} %param.29) | copy-start | bytes 24580
  0.7 14.0 %copy-start.9 = (s32[512]{0:T(512)S(1)}, s32[512]{0:T(512)}, u32[]{:S(2)}) copy-start(s32[512]{0:T(512)} %param.24) | copy-start | bytes 6148
  3.1 20.9 %all-to-all-start = ((s32[128,1,128]{2,1,0:T(1,128)}), s32[128,1,128]{2,1,0:T(1,128)S(1)}, u32[]{:S(2)}, u32[]{:S(2)}) async-start(s32[128,1,128]{2,1,0:T(1,128)} %get-tuple-element.14), calls=%async_computation | async-start | bytes 131072 | tf_op jit(solution)/shard_map/all_to_all | solution.py:425
  26.1 5.7 %copy-start.2 = (s32[8192,2]{0,1:T(2,128)S(1)}, s32[8192,2]{0,1:T(2,128)}, u32[]{:S(2)}) copy-start(s32[8192,2]{0,1:T(2,128)} %param.25) | copy-start | bytes 196612
  26.1 5.7 %copy-start.3 = (s32[8192]{0:T(1024)S(1)}, s32[8192]{0:T(1024)}, u32[]{:S(2)}) copy-start(s32[8192]{0:T(1024)} %param.26) | copy-start | bytes 98308
  26.1 5.7 %copy-start.7 = (s32[1024,2]{0,1:T(2,128)S(1)}, s32[1024,2]{0,1:T(2,128)}, u32[]{:S(2)}) copy-start(s32[1024,2]{0,1:T(2,128)} %param.20) | copy-start | bytes 24580
  26.1 5.7 %copy-start.8 = (s32[1024]{0:T(1024)S(1)}, s32[1024]{0:T(1024)}, u32[]{:S(2)}) copy-start(s32[1024]{0:T(1024)} %param.21) | copy-start | bytes 12292
  26.1 27.8 %all-to-all-start.1 = ((bf16[128,40,128]{2,1,0:T(8,128)(2,1)}), bf16[128,40,128]{2,1,0:T(8,128)(2,1)S(1)}, u32[]{:S(2)}, u32[]{:S(2)}) async-start(bf16[128,40,128]{2,1,0:T(8,128)(2,1)} %shard_map.160), calls=%async_computation.1 | async-start | bytes 2621440 | tf_op jit(solution)/shard_map/all_to_all | solution.py:462
  31.8 22.1 %copy-start = (bf16[8,64,64]{2,1,0:T(8,128)(2,1)S(1)}, bf16[8,64,64]{2,1,0:T(8,128)(2,1)}, u32[]{:S(2)}) copy-start(bf16[8,64,64]{2,1,0:T(8,128)(2,1)} %maps.1) | copy-start | bytes 196612
  31.8 22.1 %copy-start.4 = (f32[64,64]{1,0:T(8,128)S(1)}, f32[64,64]{1,0:T(8,128)}, u32[]{:S(2)}) copy-start(f32[64,64]{1,0:T(8,128)} %parent.1) | copy-start | bytes 49156

commit v5 on v4

--- a/solution.py
+++ b/solution.py
@@ -246,11 +246,15 @@
 
 
 def near_kernel(
-    ops_in, s_nf, s_nc, fm, cm, f_boxes, c_boxes, f_out, c_out, ops, kinds, kf, sel, f_sum, sems
+    ops_in, s_nf, s_nc, fm, cm, f_boxes, c_boxes, slots, f_owner, f_far, f_pos,
+    f_out, c_out, hot_owner, hot_first, hot_slot, ops, kinds, kf, sel, f_sum, sems,
 ):
     copies = operator_copies(ops_in, ops, sems)
     for copy in copies:
         copy.start()
+    hot_owner[...] = one_hot_wide((f_pos[...] // PART_CAP) * DEV + f_owner[...], 4 * DEV)
+    hot_first[...] = jnp.transpose(one_hot(f_far[0:1, :] & 255, 256))
+    hot_slot[...] = jnp.transpose(one_hot(slot_rows(slots)[0] & 255, 256))
     kinds[0:G_NEAR_F] = s_nf[...]
     kinds[G_NEAR_F:NEAR_GROUPS] = s_nc[...]
     pick_operators(copies, ops, kinds, kf, sel)
@@ -294,8 +298,8 @@
 
 
 def final_kernel(
-    got, slots, sel, f_near, c_near, parent, maps, f_owner, f_boxes, f_pos, c_owner, c_boxes, c_pos,
-    c_ref, f_ref, flat,
+    got, slots, sel, f_near, c_near, hot_owner, hot_first, hot_slot, parent, maps, f_boxes, f_pos,
+    c_owner, c_boxes, c_pos, c_ref, f_ref, flat,
 ):
     flat[...] = got[...].astype(F32).reshape(DEV * ROWS, 128)
     f_row, c_row = slot_rows(slots)
@@ -332,13 +336,12 @@
         axis=0,
     ).astype(BF16)
     pos = f_pos[...]
-    hot = one_hot_wide((pos // PART_CAP) * DEV + f_owner[...], 4 * DEV)
-    vec = choose(mm(held, hot), pos & (PART_CAP - 1), PART_CAP)
+    vec = choose(mm(held, hot_owner[...]), pos & (PART_CAP - 1), PART_CAP)
     to_1 = jnp.concatenate(
         [mm(sel[g], vec[:, g * 128:(g + 1) * 128]) for g in range(G_FAR_F)], axis=1
     )
     first = f_boxes[0:1, :]
-    total = mm_nt(spread_fine(to_1, first), one_hot(first & 255, 256))
+    total = mm(spread_fine(to_1, first), hot_first[...])
     sides = []
     for kp in range(ROWS_F):
         arrived = turned(ROWS_F + kp)
@@ -347,7 +350,7 @@
     side = jnp.concatenate(
         [jnp.where(f_row < 256, side, 0.0), jnp.where(f_row < 256, 0.0, side)], axis=0
     )
-    added = mm_nt(side.astype(BF16), one_hot(f_row & 255, 256))
+    added = mm(side.astype(BF16), hot_slot[...])
 
     box = lax.broadcasted_iota(I32, (64, 512), 1)
     parent_of = jnp.where((box >> 3) == lax.broadcasted_iota(I32, (64, 512), 0), 1.0, 0.0)
@@ -460,9 +463,15 @@
         asked, fm, cm, f_part, c_part,
     )
     got = lax.all_to_all(sent, ("oct", "box"), split_axis=0, concat_axis=0, tiled=True)
-    f_near, c_near = call(
+    f_near, c_near, hot_owner, hot_first, hot_slot = call(
         near_kernel,
-        (sds((2 * RANK, 256), F32), sds((RANK, 64), F32)),
+        (
+            pltpu.VMEM((2 * RANK, 256), F32),
+            pltpu.VMEM((RANK, 64), F32),
+            pltpu.VMEM((4 * DEV, n_f), BF16),
+            pltpu.VMEM((n_f, 256), BF16),
+            pltpu.VMEM((CAP_F * DEV, 256), BF16),
+        ),
         [
             pltpu.VMEM(ops.shape, BF16),
             pltpu.VMEM((NEAR_GROUPS, 128), I32),
@@ -477,8 +486,8 @@
         ops,
         fine_near_shift.reshape(-1, 128),
         coarse_near_shift.reshape(-1, 128),
-        fm, cm, fine_near_boxes.T, coarse_near_boxes.T,
-        in_specs=[hbm] + [vmem] * 6,
+        fm, cm, fine_near_boxes.T, coarse_near_boxes.T, asked, f_owner, f_far, f_pos,
+        in_specs=[hbm] + [vmem] * 10,
     )
     return call(
         final_kernel,
@@ -487,8 +496,8 @@
         MIB_5,
         3 * 10**9,
         10**7,
-        got, asked, sel, f_near, c_near, parent_local, child_maps,
-        f_owner, f_far, f_pos, c_owner, c_far, c_pos,
+        got, asked, sel, f_near, c_near, hot_owner, hot_first, hot_slot, parent_local, child_maps,
+        f_far, f_pos, c_owner, c_far, c_pos,
     )
 
 

time: 58.2 us -> 61.1 us (1.050)
  local copies, waits for them, and re-layouts: 0.04 us -> 5.87 us
  waiting for transfers between devices: 16 us -> 12.5 us
    unnamed x20 -> x28, local copies, waits for them, and re-layouts: 0.04 us -> 5.87 us
    all_to_all x1, waiting for transfers between devices: 11.8 us -> 8.33 us  [on_device(): lax.all_to_all(sent, ('oct', 'box'), split_axis=0, concat_axis=0, tiled=T...]
where the time goes in v5:
time: 61.1 us; the launch traced here: 60.7 us
  Pallas kernels  24.4 us (40%)
  starting transfers between devices  17.1 us (28%)
  waiting for transfers between devices  12.5 us (20%)
  local copies, waits for them, and re-layouts  5.87 us (10%)
  between operations  0.8 us (1%)
    pallas_call x5, Pallas kernels, call(): pl.pallas_call(kernel, out_shape=out_shape, scratch_shapes=scratch, compi...  24.4 us
    all_to_all x1, starting transfers between devices, on_device(): lax.all_to_all(slots, ('oct', 'box'), split_axis=0, concat_axis=0, tiled=...  11.5 us
    all_to_all x1, waiting for transfers between devices, on_device(): lax.all_to_all(sent, ('oct', 'box'), split_axis=0, concat_axis=0, tiled=T...  8.33 us
    unnamed x28, local copies, waits for them, and re-layouts  5.87 us
    all_to_all x1, starting transfers between devices, on_device(): lax.all_to_all(sent, ('oct', 'box'), split_axis=0, concat_axis=0, tiled=T...  5.65 us
    all_to_all x1, waiting for transfers between devices, on_device(): lax.all_to_all(slots, ('oct', 'box'), split_axis=0, concat_axis=0, tiled=...  4.14 us
  transfers between devices with their start and end apart: 2, of which 2 were waited for; matrix products, arithmetic and copies ran while one was open for 0% of the time, Pallas kernels for 27%

profile of v5, /device:TPU:1, one launch (start us, length us, event | category | flops | bytes accessed | tf_op | source)
XLA Modules:
  0.0 60.7 jit_solution(5187762856296840079)
XLA Ops:
  0.6 0.0 copy-start.1
  0.6 0.0 copy-start.5
  0.7 0.0 copy-start.6
  0.7 0.0 copy-start.9
  0.7 2.4 %shard_map.158 = (s32[128,1,128]{2,1,0:T(1,128)}, s32[1,2048]{1,0:T(1,128)S(1)}, s32[1,512]{1,0:T(1,128)S(1)}, s32[1,2048]{1,0:T(1,128)S(1)}, s32[2,2048]{1,0:T(...) custom-call(s32[1,2048]{1,0:T(1,128)} %bitcast.20, s32[2,2048]{1,0:T(2,128)} %bitcast.19, s32[1,512]{1,0:T(1,128)} %bitcast.22, ...), custom_call_target="tpu_custom_call" | custom-call | flops 1000000000 | bytes 1000000 | tf_op jit(solution)/shard_map/pallas_call | solution.py:369
  3.1 11.5 %all-to-all-start = ((s32[128,1,128]{2,1,0:T(1,128)}), s32[128,1,128]{2,1,0:T(1,128)S(1)}, u32[]{:S(2)}, u32[]{:S(2)}) async-start(s32[128,1,128]{2,1,0:T(1,128)} %get-tuple-element.17), calls=%async_computation | async-start | bytes 131072 | tf_op jit(solution)/shard_map/all_to_all | solution.py:428
  14.6 0.0 copy-done.1
  14.6 0.0 copy-done.5
  14.6 0.0 copy-done.6
  14.7 0.0 copy-done.9
  14.7 5.2 %shard_map.159 = (bf16[24,64,64]{2,1,0:T(8,128)(2,1)S(1)}, bf16[128,16,128]{2,1,0:T(8,128)(2,1)S(1)}, f32[4,128,128]{2,1,0:T(8,128)S(1)}) custom-call(bf16[64,64,316]{2,1,0:T(8,128)(2,1)} %bitcast.17, s32[16,128]{1,0:T(8,128)S(1)} %bitcast.13, s32[4,128]{1,0:T(4,128)S(1)} %bitcast.16, bf16[64,512]{1,0:T(8,128)(2,1)S(1)} %copy-done.1, ...), custom_call_target="tpu_custom_call" | custom-call | flops 5000000000 | bytes 10000000 | tf_op jit(solution)/shard_map/pallas_call | solution.py:369
  19.9 4.1 %all-to-all-done.slots = s32[128,1,128]{2,1,0:T(1,128)S(1)} async-done(((s32[128,1,128]{2,1,0:T(1,128)}), s32[128,1,128]{2,1,0:T(1,128)S(1)}, u32[]{:S(2)}, u32[]{:S(2)}) %all-to-all-start) | async-done | bytes 65568 | tf_op jit(solution)/shard_map/all_to_all | solution.py:428
  24.0 2.1 %shard_map.160 = bf16[128,40,128]{2,1,0:T(8,128)(2,1)} custom-call(s32[128,1,128]{2,1,0:T(1,128)S(1)} %all-to-all-done.slots, bf16[64,512]{1,0:T(8,128)(2,1)S(1)} %copy-done.1, bf16[64,64]{1,0:T(8,128)(2,1)S(1)} %copy-done.5, bf16[128,16,128]{2,1,0:T(8,128)(2,1)S(1)} %get-tuple-element.24.f_part, f32[4,128,128]{2,1,0:T(8,128)S(1)} %get-tuple-element.25.c_part), custom_call_target="tpu_custom_call" | custom-call | flops 1000000000 | bytes 1000000 | tf_op jit(solution)/shard_map/pallas_call | solution.py:369
  26.1 0.0 copy-start.2
  26.1 0.0 copy-start.3
  26.1 0.0 copy-start.7
  26.1 0.0 copy-start.8
  26.1 5.6 %all-to-all-start.1 = ((bf16[128,40,128]{2,1,0:T(8,128)(2,1)}), bf16[128,40,128]{2,1,0:T(8,128)(2,1)S(1)}, u32[]{:S(2)}, u32[]{:S(2)}) async-start(bf16[128,40,128]{2,1,0:T(8,128)(2,1)} %shard_map.160), calls=%async_computation.1 | async-start | bytes 2621440 | tf_op jit(solution)/shard_map/all_to_all | solution.py:465
  31.8 0.0 copy-done.2
  31.8 0.0 copy-done.3
  31.8 0.0 copy-done.7
  31.8 0.0 copy-done.8
  31.8 0.0 copy-start
  31.8 0.0 copy-start.4
  31.9 11.1 %shard_map.161 = (f32[128,256]{1,0:T(8,128)S(1)}, f32[64,64]{1,0:T(8,128)S(1)}, bf16[512,2048]{1,0:T(8,128)(2,1)S(1)}, bf16[2048,256]{1,0:T(8,128)(2,1)S(1)}, bf16[4096,256]{1,0:T(8,128)(2,1)S(1)}) custom-call(bf16[64,64,316]{2,1,0:T(8,128)(2,1)} %bitcast.18, s32[64,128]{1,0:T(8,128)S(1)} %bitcast.12, s32[8,128]{1,0:T(8,128)S(1)} %bitcast.15, ...), custom_call_target="tpu_custom_call" | custom-call | flops 10000000000 | bytes 10000000 | tf_op jit(solution)/shard_map/pallas_call | solution.py:369
  43.0 0.0 copy-start.10
  43.0 1.3 %copy-done.10 = bf16[512,2048]{1,0:T(8,128)(2,1)} copy-done((bf16[512,2048]{1,0:T(8,128)(2,1)}, bf16[512,2048]{1,0:T(8,128)(2,1)S(1)}, u32[]{:S(2)}) %copy-start.10) | copy-done | bytes 2097176
  44.3 0.0 copy-start.12
  44.3 1.3 %copy-done.12 = bf16[4096,256]{1,0:T(8,128)(2,1)} copy-done((bf16[4096,256]{1,0:T(8,128)(2,1)}, bf16[4096,256]{1,0:T(8,128)(2,1)S(1)}, u32[]{:S(2)}) %copy-start.12) | copy-done | bytes 2097176
  45.6 8.3 %all-to-all-done.1.got = bf16[128,40,128]{2,1,0:T(8,128)(2,1)S(1)} async-done(((bf16[128,40,128]{2,1,0:T(8,128)(2,1)}), bf16[128,40,128]{2,1,0:T(8,128)(2,1)S(1)}, u32[]{:S(2)}, u32[]{:S(2)}) %all-to-all-start.1) | async-done | bytes 1310752 | tf_op jit(solution)/shard_map/all_to_all | solution.py:465
  53.9 0.0 copy-done
  53.9 0.0 copy-done.4
  53.9 0.0 copy-start.11
  53.9 1.6 %copy-done.11 = bf16[512,2048]{1,0:T(8,128)(2,1)S(1)} copy-done((bf16[512,2048]{1,0:T(8,128)(2,1)S(1)}, bf16[512,2048]{1,0:T(8,128)(2,1)}, u32[]{:S(2)}) %copy-start.11) | copy-done | bytes 2097176
  55.5 0.0 copy-start.13
  55.5 1.6 %copy-done.13 = bf16[4096,256]{1,0:T(8,128)(2,1)S(1)} copy-done((bf16[4096,256]{1,0:T(8,128)(2,1)S(1)}, bf16[4096,256]{1,0:T(8,128)(2,1)}, u32[]{:S(2)}) %copy-start.13) | copy-done | bytes 2097176
  57.1 3.6 %shard_map.162 = (bf16[64,64]{1,0:T(8,128)(2,1)}, bf16[64,512]{1,0:T(8,128)(2,1)}) custom-call(bf16[128,40,128]{2,1,0:T(8,128)(2,1)S(1)} %all-to-all-done.1.got, s32[128,1,128]{2,1,0:T(1,128)S(1)} %all-to-all-done.slots, bf16[24,64,64]{2,1,0:T(8,128)(2,1)S(1)} %get-tuple-element.26.sel, f32[128,256]{1,0:T(8,128)S(1)} %get-tuple-element.27.f_near, ...), custom_call_target="tpu_custom_call" | custom-call | flops 3000000000 | bytes 10000000 | tf_op jit(solution)/shard_map/pallas_call | solution.py:369
Async XLA Ops:
  0.6 14.0 %copy-start.1 = (bf16[64,512]{1,0:T(8,128)(2,1)S(1)}, bf16[64,512]{1,0:T(8,128)(2,1)}, u32[]{:S(2)}) copy-start(bf16[64,512]{1,0:T(8,128)(2,1)} %fm.5) | copy-start | bytes 196612
  0.6 14.0 %copy-start.5 = (bf16[64,64]{1,0:T(8,128)(2,1)S(1)}, bf16[64,64]{1,0:T(8,128)(2,1)}, u32[]{:S(2)}) copy-start(bf16[64,64]{1,0:T(8,128)(2,1)} %cm.5) | copy-start | bytes 24580
  0.7 14.0 %copy-start.6 = (s32[2048]{0:T(1024)S(1)}, s32[2048]{0:T(1024)}, u32[]{:S(2)}) copy-start(s32[2048]{0:T(1024)} %param.29) | copy-start | bytes 24580
  0.7 14.0 %copy-start.9 = (s32[512]{0:T(512)S(1)}, s32[512]{0:T(512)}, u32[]{:S(2)}) copy-start(s32[512]{0:T(512)} %param.24) | copy-start | bytes 6148
  3.1 20.9 %all-to-all-start = ((s32[128,1,128]{2,1,0:T(1,128)}), s32[128,1,128]{2,1,0:T(1,128)S(1)}, u32[]{:S(2)}, u32[]{:S(2)}) async-start(s32[128,1,128]{2,1,0:T(1,128)} %get-tuple-element.17), calls=%async_computation | async-start | bytes 131072 | tf_op jit(solution)/shard_map/all_to_all | solution.py:428
  26.1 5.7 %copy-start.2 = (s32[8192,2]{0,1:T(2,128)S(1)}, s32[8192,2]{0,1:T(2,128)}, u32[]{:S(2)}) copy-start(s32[8192,2]{0,1:T(2,128)} %param.25) | copy-start | bytes 196612
  26.1 5.7 %copy-start.3 = (s32[8192]{0:T(1024)S(1)}, s32[8192]{0:T(1024)}, u32[]{:S(2)}) copy-start(s32[8192]{0:T(1024)} %param.26) | copy-start | bytes 98308
  26.1 5.7 %copy-start.7 = (s32[1024,2]{0,1:T(2,128)S(1)}, s32[1024,2]{0,1:T(2,128)}, u32[]{:S(2)}) copy-start(s32[1024,2]{0,1:T(2,128)} %param.20) | copy-start | bytes 24580
  26.1 5.7 %copy-start.8 = (s32[1024]{0:T(1024)S(1)}, s32[1024]{0:T(1024)}, u32[]{:S(2)}) copy-start(s32[1024]{0:T(1024)} %param.21) | copy-start | bytes 12292
  26.1 27.8 %all-to-all-start.1 = ((bf16[128,40,128]{2,1,0:T(8,128)(2,1)}), bf16[128,40,128]{2,1,0:T(8,128)(2,1)S(1)}, u32[]{:S(2)}, u32[]{:S(2)}) async-start(bf16[128,40,128]{2,1,0:T(8,128)(2,1)} %shard_map.160), calls=%async_computation.1 | async-start | bytes 2621440 | tf_op jit(solution)/shard_map/all_to_all | solution.py:465
  31.8 22.1 %copy-start = (bf16[8,64,64]{2,1,0:T(8,128)(2,1)S(1)}, bf16[8,64,64]{2,1,0:T(8,128)(2,1)}, u32[]{:S(2)}) copy-start(bf16[8,64,64]{2,1,0:T(8,128)(2,1)} %maps.1) | copy-start | bytes 196612
  31.8 22.1 %copy-start.4 = (f32[64,64]{1,0:T(8,128)S(1)}, f32[64,64]{1,0:T(8,128)}, u32[]{:S(2)}) copy-start(f32[64,64]{1,0:T(8,128)} %parent.1) | copy-start | bytes 49156
  43.0 1.3 %copy-start.10 = (bf16[512,2048]{1,0:T(8,128)(2,1)}, bf16[512,2048]{1,0:T(8,128)(2,1)S(1)}, u32[]{:S(2)}) copy-start(bf16[512,2048]{1,0:T(8,128)(2,1)S(1)} %get-tuple-element.29.hot_owner) | copy-start | bytes 6291460
  44.3 1.3 %copy-start.12 = (bf16[4096,256]{1,0:T(8,128)(2,1)}, bf16[4096,256]{1,0:T(8,128)(2,1)S(1)}, u32[]{:S(2)}) copy-start(bf16[4096,256]{1,0:T(8,128)(2,1)S(1)} %get-tuple-element.31.hot_slot) | copy-start | bytes 6291460
  53.9 1.6 %copy-start.11 = (bf16[512,2048]{1,0:T(8,128)(2,1)S(1)}, bf16[512,2048]{1,0:T(8,128)(2,1)}, u32[]{:S(2)}) copy-start(bf16[512,2048]{1,0:T(8,128)(2,1)} %copy-done.10) | copy-start | bytes 6291460
  55.5 1.6 %copy-start.13 = (bf16[4096,256]{1,0:T(8,128)(2,1)S(1)}, bf16[4096,256]{1,0:T(8,128)(2,1)}, u32[]{:S(2)}) copy-start(bf16[4096,256]{1,0:T(8,128)(2,1)} %copy-done.12) | copy-start | bytes 6291460

commit v6 on v4

--- a/solution.py
+++ b/solution.py
@@ -25,6 +25,7 @@
 NEAR_BLOCK = 4096
 PM_ROWS = 512
 OPS_CHUNKS = 2
+SENDS = 4
 MIB_1, MIB_2, MIB_3, MIB_4, MIB_5 = 16, 36, 24, 44, 40
 
 
@@ -75,9 +76,9 @@
 
 
 def prefix_matrix():
-    down = lax.broadcasted_iota(I32, (128, 256), 0)
-    across = lax.broadcasted_iota(I32, (128, 256), 1)
-    return jnp.where((down <= across) | (across >= 128), 1.0, 0.0).astype(BF16)
+    down = lax.broadcasted_iota(I32, (128, 128), 0)
+    across = lax.broadcasted_iota(I32, (128, 128), 1)
+    return jnp.where(down <= across, 1.0, 0.0).astype(BF16)
 
 
 def route_kernel(
@@ -114,9 +115,9 @@
         for b in range(blocks):
             lanes = slice(b * 128, (b + 1) * 128)
             count = counts[(start + b) * 128:(start + b + 1) * 128]
-            seen = count[:, :128] + carry
+            seen = count + carry
             pos = jnp.sum(jnp.where(hits[start + b], seen, 0.0), axis=0, keepdims=True) - 1.0
-            carry = carry + count[:, 128:]
+            carry = carry + jnp.broadcast_to(count[:, 127:128], (DEV, 128))
             pos = pos.astype(I32)
             pos_ref[:, lanes] = pos
             slot = boxes_ref[1:2, lanes]
@@ -219,7 +220,7 @@
     return jnp.concatenate(rows[:CAP_F], axis=1), jnp.concatenate(rows[CAP_F:], axis=1)
 
 
-def reply_kernel(slots, fm, cm, f_part, c_part, out_ref, f_flat, c_flat):
+def reply_kernel(slots, fm, cm, f_part, c_part, out_ref, f_flat, c_flat, stage, sems):
     f_row, c_row = slot_rows(slots)
     f_vec = pick_fine(half_stack(fm[...]), one_hot(f_row & 255, 256), f_row)
     c_vec = mm(cm[...], one_hot(c_row, 64))
@@ -235,14 +236,24 @@
     for kp in range(ROWS_C):
         c_flat[pl.ds(kp, DEV, stride=2 * ROWS_C), :] = turned(c_vec, kp)
         c_flat[pl.ds(ROWS_C + kp, DEV, stride=2 * ROWS_C), :] = c_part[kp]
-    out_ref[...] = jnp.concatenate(
-        [
-            f_flat[...].reshape(DEV, ROWS_F, 128).astype(BF16),
-            f_part[...],
-            c_flat[...].reshape(DEV, 2 * ROWS_C, 128).astype(BF16),
-        ],
-        axis=1,
-    )
+    each = DEV // SENDS
+    copies = []
+    for q in range(SENDS):
+        devices = pl.ds(q * each, each)
+        f_rows = f_flat[pl.ds(q * each * ROWS_F, each * ROWS_F), :]
+        c_rows = c_flat[pl.ds(q * each * 2 * ROWS_C, each * 2 * ROWS_C), :]
+        stage[devices] = jnp.concatenate(
+            [
+                f_rows.reshape(each, ROWS_F, 128).astype(BF16),
+                f_part[devices],
+                c_rows.reshape(each, 2 * ROWS_C, 128).astype(BF16),
+            ],
+            axis=1,
+        )
+        copies.append(pltpu.make_async_copy(stage.at[devices], out_ref.at[devices], sems.at[q]))
+        copies[-1].start()
+    for copy in copies:
+        copy.wait()
 
 
 def near_kernel(
@@ -452,12 +463,19 @@
     )
     sent = call(
         reply_kernel,
-        sds((DEV, ROWS, 128), BF16),
-        [pltpu.VMEM((DEV * ROWS_F, 128), F32), pltpu.VMEM((DEV * 2 * ROWS_C, 128), F32)],
+        pltpu.HBM((DEV, ROWS, 128), BF16),
+        [
+            pltpu.VMEM((DEV * ROWS_F, 128), F32),
+            pltpu.VMEM((DEV * 2 * ROWS_C, 128), F32),
+            pltpu.VMEM((DEV, ROWS, 128), BF16),
+            pltpu.SemaphoreType.DMA((SENDS,)),
+        ],
         MIB_3,
         10**9,
         10**6,
         asked, fm, cm, f_part, c_part,
+        in_specs=[vmem] * 5,
+        out_specs=hbm,
     )
     got = lax.all_to_all(sent, ("oct", "box"), split_axis=0, concat_axis=0, tiled=True)
     f_near, c_near = call(

time: 58.2 us -> 58 us (level)
  no operation moved by 1% of the time
where the time goes in v6:
time: 58 us; the launch traced here: 57.7 us
  Pallas kernels  23.7 us (41%)
  starting transfers between devices  17.1 us (29%)
  waiting for transfers between devices  15.9 us (27%)
  between operations  0.82 us (1%)
    pallas_call x5, Pallas kernels, call(): pl.pallas_call(kernel, out_shape=out_shape, scratch_shapes=scratch, compi...  23.7 us
    all_to_all x1, waiting for transfers between devices, on_device(): lax.all_to_all(sent, ('oct', 'box'), split_axis=0, concat_axis=0, tiled=T...  11.8 us
    all_to_all x1, starting transfers between devices, on_device(): lax.all_to_all(slots, ('oct', 'box'), split_axis=0, concat_axis=0, tiled=...  11.5 us
    all_to_all x1, starting transfers between devices, on_device(): lax.all_to_all(sent, ('oct', 'box'), split_axis=0, concat_axis=0, tiled=T...  5.64 us
    all_to_all x1, waiting for transfers between devices, on_device(): lax.all_to_all(slots, ('oct', 'box'), split_axis=0, concat_axis=0, tiled=...  4.14 us
  transfers between devices with their start and end apart: 2, of which 2 were waited for; matrix products, arithmetic and copies ran while one was open for 0% of the time, Pallas kernels for 27%

profile of v6, /device:TPU:1, one launch (start us, length us, event | category | flops | bytes accessed | tf_op | source)
XLA Modules:
  0.0 57.7 jit_solution(17600929401704142213)
XLA Ops:
  0.6 0.0 copy-start.1
  0.6 0.0 copy-start.5
  0.7 0.0 copy-start.6
  0.7 0.0 copy-start.9
  0.7 2.3 %shard_map.158 = (s32[128,1,128]{2,1,0:T(1,128)}, s32[1,2048]{1,0:T(1,128)S(1)}, s32[1,512]{1,0:T(1,128)S(1)}, s32[1,2048]{1,0:T(1,128)S(1)}, s32[2,2048]{1,0:T(...) custom-call(s32[1,2048]{1,0:T(1,128)} %bitcast.20, s32[2,2048]{1,0:T(2,128)} %bitcast.19, s32[1,512]{1,0:T(1,128)} %bitcast.22, ...), custom_call_target="tpu_custom_call" | custom-call | flops 1000000000 | bytes 1000000 | tf_op jit(solution)/shard_map/pallas_call | solution.py:377
  3.0 11.5 %all-to-all-start = ((s32[128,1,128]{2,1,0:T(1,128)}), s32[128,1,128]{2,1,0:T(1,128)S(1)}, u32[]{:S(2)}, u32[]{:S(2)}) async-start(s32[128,1,128]{2,1,0:T(1,128)} %get-tuple-element.14), calls=%async_computation | async-start | bytes 131072 | tf_op jit(solution)/shard_map/all_to_all | solution.py:436
  14.5 0.0 copy-done.1
  14.5 0.0 copy-done.5
  14.5 0.0 copy-done.6
  14.5 0.0 copy-done.9
  14.5 5.2 %shard_map.159 = (bf16[24,64,64]{2,1,0:T(8,128)(2,1)S(1)}, bf16[128,16,128]{2,1,0:T(8,128)(2,1)S(1)}, f32[4,128,128]{2,1,0:T(8,128)S(1)}) custom-call(bf16[64,64,316]{2,1,0:T(8,128)(2,1)} %bitcast.17, s32[16,128]{1,0:T(8,128)S(1)} %bitcast.13, s32[4,128]{1,0:T(4,128)S(1)} %bitcast.16, bf16[64,512]{1,0:T(8,128)(2,1)S(1)} %copy-done.1, ...), custom_call_target="tpu_custom_call" | custom-call | flops 5000000000 | bytes 10000000 | tf_op jit(solution)/shard_map/pallas_call | solution.py:377
  19.8 4.1 %all-to-all-done.slots = s32[128,1,128]{2,1,0:T(1,128)S(1)} async-done(((s32[128,1,128]{2,1,0:T(1,128)}), s32[128,1,128]{2,1,0:T(1,128)S(1)}, u32[]{:S(2)}, u32[]{:S(2)}) %all-to-all-start) | async-done | bytes 65568 | tf_op jit(solution)/shard_map/all_to_all | solution.py:436
  23.9 2.0 %shard_map.160 = bf16[128,40,128]{2,1,0:T(8,128)(2,1)} custom-call(s32[128,1,128]{2,1,0:T(1,128)S(1)} %all-to-all-done.slots, bf16[64,512]{1,0:T(8,128)(2,1)S(1)} %copy-done.1, bf16[64,64]{1,0:T(8,128)(2,1)S(1)} %copy-done.5, bf16[128,16,128]{2,1,0:T(8,128)(2,1)S(1)} %get-tuple-element.21.f_part, f32[4,128,128]{2,1,0:T(8,128)S(1)} %get-tuple-element.22.c_part), custom_call_target="tpu_custom_call" | custom-call | flops 1000000000 | bytes 1000000 | tf_op jit(solution)/shard_map/pallas_call | solution.py:377
  25.9 0.0 copy-start.2
  25.9 0.0 copy-start.3
  25.9 0.0 copy-start.7
  25.9 0.0 copy-start.8
  25.9 5.6 %all-to-all-start.1 = ((bf16[128,40,128]{2,1,0:T(8,128)(2,1)}), bf16[128,40,128]{2,1,0:T(8,128)(2,1)S(1)}, u32[]{:S(2)}, u32[]{:S(2)}) async-start(bf16[128,40,128]{2,1,0:T(8,128)(2,1)} %shard_map.160), calls=%async_computation.1 | async-start | bytes 2621440 | tf_op jit(solution)/shard_map/all_to_all | solution.py:480
  31.6 0.0 copy-done.2
  31.6 0.0 copy-done.3
  31.6 0.0 copy-done.7
  31.6 0.0 copy-done.8
  31.6 0.0 copy-start
  31.6 0.0 copy-start.4
  31.6 10.3 %shard_map.161 = (f32[128,256]{1,0:T(8,128)S(1)}, f32[64,64]{1,0:T(8,128)S(1)}) custom-call(bf16[64,64,316]{2,1,0:T(8,128)(2,1)} %bitcast.18, s32[64,128]{1,0:T(8,128)S(1)} %bitcast.12, s32[8,128]{1,0:T(8,128)S(1)} %bitcast.15, bf16[64,512]{1,0:T(8,128)(2,1)S(1)} %copy-done.1, bf16[64,64]{1,0:T(8,128)(2,1)S(1)} %copy-done.5, s32[2,8192]{1,0:T(2,128)S(1)} %bitcast.11, ...), custom_call_target="tpu_custom_call" | custom-call | flops 10000000000 | bytes 10000000 | tf_op jit(solution)/shard_map/pallas_call | solution.py:377
  41.9 11.8 %all-to-all-done.1.got = bf16[128,40,128]{2,1,0:T(8,128)(2,1)S(1)} async-done(((bf16[128,40,128]{2,1,0:T(8,128)(2,1)}), bf16[128,40,128]{2,1,0:T(8,128)(2,1)S(1)}, u32[]{:S(2)}, u32[]{:S(2)}) %all-to-all-start.1) | async-done | bytes 1310752 | tf_op jit(solution)/shard_map/all_to_all | solution.py:480
  53.7 0.0 copy-done
  53.7 0.0 copy-done.4
  53.7 4.0 %shard_map.162 = (bf16[64,64]{1,0:T(8,128)(2,1)}, bf16[64,512]{1,0:T(8,128)(2,1)}) custom-call(bf16[128,40,128]{2,1,0:T(8,128)(2,1)S(1)} %all-to-all-done.1.got, s32[128,1,128]{2,1,0:T(1,128)S(1)} %all-to-all-done.slots, bf16[24,64,64]{2,1,0:T(8,128)(2,1)S(1)} %get-tuple-element.23.sel, f32[128,256]{1,0:T(8,128)S(1)} %get-tuple-element.24.f_near, ...), custom_call_target="tpu_custom_call" | custom-call | flops 3000000000 | bytes 10000000 | tf_op jit(solution)/shard_map/pallas_call | solution.py:377
Async XLA Ops:
  0.6 13.9 %copy-start.1 = (bf16[64,512]{1,0:T(8,128)(2,1)S(1)}, bf16[64,512]{1,0:T(8,128)(2,1)}, u32[]{:S(2)}) copy-start(bf16[64,512]{1,0:T(8,128)(2,1)} %fm.5) | copy-start | bytes 196612
  0.6 13.9 %copy-start.5 = (bf16[64,64]{1,0:T(8,128)(2,1)S(1)}, bf16[64,64]{1,0:T(8,128)(2,1)}, u32[]{:S(2)}) copy-start(bf16[64,64]{1,0:T(8,128)(2,1)} %cm.5) | copy-start | bytes 24580
  0.7 13.9 %copy-start.6 = (s32[2048]{0:T(1024)S(1)}, s32[2048]{0:T(1024)}, u32[]{:S(2)}) copy-start(s32[2048]{0:T(1024)} %param.29) | copy-start | bytes 24580
  0.7 13.9 %copy-start.9 = (s32[512]{0:T(512)S(1)}, s32[512]{0:T(512)}, u32[]{:S(2)}) copy-start(s32[512]{0:T(512)} %param.24) | copy-start | bytes 6148
  3.0 20.9 %all-to-all-start = ((s32[128,1,128]{2,1,0:T(1,128)}), s32[128,1,128]{2,1,0:T(1,128)S(1)}, u32[]{:S(2)}, u32[]{:S(2)}) async-start(s32[128,1,128]{2,1,0:T(1,128)} %get-tuple-element.14), calls=%async_computation | async-start | bytes 131072 | tf_op jit(solution)/shard_map/all_to_all | solution.py:436
  25.9 5.7 %copy-start.2 = (s32[8192,2]{0,1:T(2,128)S(1)}, s32[8192,2]{0,1:T(2,128)}, u32[]{:S(2)}) copy-start(s32[8192,2]{0,1:T(2,128)} %param.25) | copy-start | bytes 196612
  25.9 5.7 %copy-start.3 = (s32[8192]{0:T(1024)S(1)}, s32[8192]{0:T(1024)}, u32[]{:S(2)}) copy-start(s32[8192]{0:T(1024)} %param.26) | copy-start | bytes 98308
  25.9 5.7 %copy-start.7 = (s32[1024,2]{0,1:T(2,128)S(1)}, s32[1024,2]{0,1:T(2,128)}, u32[]{:S(2)}) copy-start(s32[1024,2]{0,1:T(2,128)} %param.20) | copy-start | bytes 24580
  25.9 5.7 %copy-start.8 = (s32[1024]{0:T(1024)S(1)}, s32[1024]{0:T(1024)}, u32[]{:S(2)}) copy-start(s32[1024]{0:T(1024)} %param.21) | copy-start | bytes 12292
  25.9 27.8 %all-to-all-start.1 = ((bf16[128,40,128]{2,1,0:T(8,128)(2,1)}), bf16[128,40,128]{2,1,0:T(8,128)(2,1)S(1)}, u32[]{:S(2)}, u32[]{:S(2)}) async-start(bf16[128,40,128]{2,1,0:T(8,128)(2,1)} %shard_map.160), calls=%async_computation.1 | async-start | bytes 2621440 | tf_op jit(solution)/shard_map/all_to_all | solution.py:480
  31.6 22.1 %copy-start = (bf16[8,64,64]{2,1,0:T(8,128)(2,1)S(1)}, bf16[8,64,64]{2,1,0:T(8,128)(2,1)}, u32[]{:S(2)}) copy-start(bf16[8,64,64]{2,1,0:T(8,128)(2,1)} %maps.1) | copy-start | bytes 196612
  31.6 22.1 %copy-start.4 = (f32[64,64]{1,0:T(8,128)S(1)}, f32[64,64]{1,0:T(8,128)}, u32[]{:S(2)}) copy-start(f32[64,64]{1,0:T(8,128)} %parent.1) | copy-start | bytes 49156

commit v7 on v6

--- a/solution.py
+++ b/solution.py
@@ -25,7 +25,7 @@
 NEAR_BLOCK = 4096
 PM_ROWS = 512
 OPS_CHUNKS = 2
-SENDS = 4
+SENDS = 8
 MIB_1, MIB_2, MIB_3, MIB_4, MIB_5 = 16, 36, 24, 44, 40
 
 

time: 58 us -> 58 us (level)
  no operation moved by 1% of the time
where the time goes in v7:
time: 58 us; the launch traced here: 57.7 us
  Pallas kernels  23.7 us (41%)
  starting transfers between devices  17.1 us (29%)
  waiting for transfers between devices  15.9 us (27%)
  between operations  0.82 us (1%)
    pallas_call x5, Pallas kernels, call(): pl.pallas_call(kernel, out_shape=out_shape, scratch_shapes=scratch, compi...  23.7 us
    all_to_all x1, waiting for transfers between devices, on_device(): lax.all_to_all(sent, ('oct', 'box'), split_axis=0, concat_axis=0, tiled=T...  11.8 us
    all_to_all x1, starting transfers between devices, on_device(): lax.all_to_all(slots, ('oct', 'box'), split_axis=0, concat_axis=0, tiled=...  11.5 us
    all_to_all x1, starting transfers between devices, on_device(): lax.all_to_all(sent, ('oct', 'box'), split_axis=0, concat_axis=0, tiled=T...  5.64 us
    all_to_all x1, waiting for transfers between devices, on_device(): lax.all_to_all(slots, ('oct', 'box'), split_axis=0, concat_axis=0, tiled=...  4.14 us
  transfers between devices with their start and end apart: 2, of which 2 were waited for; matrix products, arithmetic and copies ran while one was open for 0% of the time, Pallas kernels for 27%

profile of v7, /device:TPU:1, one launch (start us, length us, event | category | flops | bytes accessed | tf_op | source)
XLA Modules:
  0.0 57.7 jit_solution(15454884035884989141)
XLA Ops:
  0.6 0.0 copy-start.1
  0.6 0.0 copy-start.5
  0.7 0.0 copy-start.6
  0.7 0.0 copy-start.9
  0.7 2.3 %shard_map.158 = (s32[128,1,128]{2,1,0:T(1,128)}, s32[1,2048]{1,0:T(1,128)S(1)}, s32[1,512]{1,0:T(1,128)S(1)}, s32[1,2048]{1,0:T(1,128)S(1)}, s32[2,2048]{1,0:T(...) custom-call(s32[1,2048]{1,0:T(1,128)} %bitcast.20, s32[2,2048]{1,0:T(2,128)} %bitcast.19, s32[1,512]{1,0:T(1,128)} %bitcast.22, ...), custom_call_target="tpu_custom_call" | custom-call | flops 1000000000 | bytes 1000000 | tf_op jit(solution)/shard_map/pallas_call | solution.py:377
  3.0 11.5 %all-to-all-start = ((s32[128,1,128]{2,1,0:T(1,128)}), s32[128,1,128]{2,1,0:T(1,128)S(1)}, u32[]{:S(2)}, u32[]{:S(2)}) async-start(s32[128,1,128]{2,1,0:T(1,128)} %get-tuple-element.14), calls=%async_computation | async-start | bytes 131072 | tf_op jit(solution)/shard_map/all_to_all | solution.py:436
  14.5 0.0 copy-done.1
  14.5 0.0 copy-done.5
  14.5 0.0 copy-done.6
  14.5 0.0 copy-done.9
  14.5 5.2 %shard_map.159 = (bf16[24,64,64]{2,1,0:T(8,128)(2,1)S(1)}, bf16[128,16,128]{2,1,0:T(8,128)(2,1)S(1)}, f32[4,128,128]{2,1,0:T(8,128)S(1)}) custom-call(bf16[64,64,316]{2,1,0:T(8,128)(2,1)} %bitcast.17, s32[16,128]{1,0:T(8,128)S(1)} %bitcast.13, s32[4,128]{1,0:T(4,128)S(1)} %bitcast.16, bf16[64,512]{1,0:T(8,128)(2,1)S(1)} %copy-done.1, ...), custom_call_target="tpu_custom_call" | custom-call | flops 5000000000 | bytes 10000000 | tf_op jit(solution)/shard_map/pallas_call | solution.py:377
  19.8 4.1 %all-to-all-done.slots = s32[128,1,128]{2,1,0:T(1,128)S(1)} async-done(((s32[128,1,128]{2,1,0:T(1,128)}), s32[128,1,128]{2,1,0:T(1,128)S(1)}, u32[]{:S(2)}, u32[]{:S(2)}) %all-to-all-start) | async-done | bytes 65568 | tf_op jit(solution)/shard_map/all_to_all | solution.py:436
  23.9 2.0 %shard_map.160 = bf16[128,40,128]{2,1,0:T(8,128)(2,1)} custom-call(s32[128,1,128]{2,1,0:T(1,128)S(1)} %all-to-all-done.slots, bf16[64,512]{1,0:T(8,128)(2,1)S(1)} %copy-done.1, bf16[64,64]{1,0:T(8,128)(2,1)S(1)} %copy-done.5, bf16[128,16,128]{2,1,0:T(8,128)(2,1)S(1)} %get-tuple-element.21.f_part, f32[4,128,128]{2,1,0:T(8,128)S(1)} %get-tuple-element.22.c_part), custom_call_target="tpu_custom_call" | custom-call | flops 1000000000 | bytes 1000000 | tf_op jit(solution)/shard_map/pallas_call | solution.py:377
  25.9 0.0 copy-start.2
  25.9 0.0 copy-start.3
  25.9 0.0 copy-start.7
  25.9 0.0 copy-start.8
  25.9 5.6 %all-to-all-start.1 = ((bf16[128,40,128]{2,1,0:T(8,128)(2,1)}), bf16[128,40,128]{2,1,0:T(8,128)(2,1)S(1)}, u32[]{:S(2)}, u32[]{:S(2)}) async-start(bf16[128,40,128]{2,1,0:T(8,128)(2,1)} %shard_map.160), calls=%async_computation.1 | async-start | bytes 2621440 | tf_op jit(solution)/shard_map/all_to_all | solution.py:480
  31.6 0.0 copy-done.2
  31.6 0.0 copy-done.3
  31.6 0.0 copy-done.7
  31.6 0.0 copy-done.8
  31.6 0.0 copy-start
  31.6 0.0 copy-start.4
  31.6 10.3 %shard_map.161 = (f32[128,256]{1,0:T(8,128)S(1)}, f32[64,64]{1,0:T(8,128)S(1)}) custom-call(bf16[64,64,316]{2,1,0:T(8,128)(2,1)} %bitcast.18, s32[64,128]{1,0:T(8,128)S(1)} %bitcast.12, s32[8,128]{1,0:T(8,128)S(1)} %bitcast.15, bf16[64,512]{1,0:T(8,128)(2,1)S(1)} %copy-done.1, bf16[64,64]{1,0:T(8,128)(2,1)S(1)} %copy-done.5, s32[2,8192]{1,0:T(2,128)S(1)} %bitcast.11, ...), custom_call_target="tpu_custom_call" | custom-call | flops 10000000000 | bytes 10000000 | tf_op jit(solution)/shard_map/pallas_call | solution.py:377
  41.9 11.8 %all-to-all-done.1.got = bf16[128,40,128]{2,1,0:T(8,128)(2,1)S(1)} async-done(((bf16[128,40,128]{2,1,0:T(8,128)(2,1)}), bf16[128,40,128]{2,1,0:T(8,128)(2,1)S(1)}, u32[]{:S(2)}, u32[]{:S(2)}) %all-to-all-start.1) | async-done | bytes 1310752 | tf_op jit(solution)/shard_map/all_to_all | solution.py:480
  53.7 0.0 copy-done
  53.7 0.0 copy-done.4
  53.7 4.0 %shard_map.162 = (bf16[64,64]{1,0:T(8,128)(2,1)}, bf16[64,512]{1,0:T(8,128)(2,1)}) custom-call(bf16[128,40,128]{2,1,0:T(8,128)(2,1)S(1)} %all-to-all-done.1.got, s32[128,1,128]{2,1,0:T(1,128)S(1)} %all-to-all-done.slots, bf16[24,64,64]{2,1,0:T(8,128)(2,1)S(1)} %get-tuple-element.23.sel, f32[128,256]{1,0:T(8,128)S(1)} %get-tuple-element.24.f_near, ...), custom_call_target="tpu_custom_call" | custom-call | flops 3000000000 | bytes 10000000 | tf_op jit(solution)/shard_map/pallas_call | solution.py:377
Async XLA Ops:
  0.6 13.9 %copy-start.1 = (bf16[64,512]{1,0:T(8,128)(2,1)S(1)}, bf16[64,512]{1,0:T(8,128)(2,1)}, u32[]{:S(2)}) copy-start(bf16[64,512]{1,0:T(8,128)(2,1)} %fm.5) | copy-start | bytes 196612
  0.6 13.9 %copy-start.5 = (bf16[64,64]{1,0:T(8,128)(2,1)S(1)}, bf16[64,64]{1,0:T(8,128)(2,1)}, u32[]{:S(2)}) copy-start(bf16[64,64]{1,0:T(8,128)(2,1)} %cm.5) | copy-start | bytes 24580
  0.7 13.9 %copy-start.6 = (s32[2048]{0:T(1024)S(1)}, s32[2048]{0:T(1024)}, u32[]{:S(2)}) copy-start(s32[2048]{0:T(1024)} %param.29) | copy-start | bytes 24580
  0.7 13.9 %copy-start.9 = (s32[512]{0:T(512)S(1)}, s32[512]{0:T(512)}, u32[]{:S(2)}) copy-start(s32[512]{0:T(512)} %param.24) | copy-start | bytes 6148
  3.0 20.9 %all-to-all-start = ((s32[128,1,128]{2,1,0:T(1,128)}), s32[128,1,128]{2,1,0:T(1,128)S(1)}, u32[]{:S(2)}, u32[]{:S(2)}) async-start(s32[128,1,128]{2,1,0:T(1,128)} %get-tuple-element.14), calls=%async_computation | async-start | bytes 131072 | tf_op jit(solution)/shard_map/all_to_all | solution.py:436
  25.9 5.7 %copy-start.2 = (s32[8192,2]{0,1:T(2,128)S(1)}, s32[8192,2]{0,1:T(2,128)}, u32[]{:S(2)}) copy-start(s32[8192,2]{0,1:T(2,128)} %param.25) | copy-start | bytes 196612
  25.9 5.7 %copy-start.3 = (s32[8192]{0:T(1024)S(1)}, s32[8192]{0:T(1024)}, u32[]{:S(2)}) copy-start(s32[8192]{0:T(1024)} %param.26) | copy-start | bytes 98308
  25.9 5.7 %copy-start.7 = (s32[1024,2]{0,1:T(2,128)S(1)}, s32[1024,2]{0,1:T(2,128)}, u32[]{:S(2)}) copy-start(s32[1024,2]{0,1:T(2,128)} %param.20) | copy-start | bytes 24580
  25.9 5.7 %copy-start.8 = (s32[1024]{0:T(1024)S(1)}, s32[1024]{0:T(1024)}, u32[]{:S(2)}) copy-start(s32[1024]{0:T(1024)} %param.21) | copy-start | bytes 12292
  25.9 27.8 %all-to-all-start.1 = ((bf16[128,40,128]{2,1,0:T(8,128)(2,1)}), bf16[128,40,128]{2,1,0:T(8,128)(2,1)S(1)}, u32[]{:S(2)}, u32[]{:S(2)}) async-start(bf16[128,40,128]{2,1,0:T(8,128)(2,1)} %shard_map.160), calls=%async_computation.1 | async-start | bytes 2621440 | tf_op jit(solution)/shard_map/all_to_all | solution.py:480
  31.6 22.1 %copy-start = (bf16[8,64,64]{2,1,0:T(8,128)(2,1)S(1)}, bf16[8,64,64]{2,1,0:T(8,128)(2,1)}, u32[]{:S(2)}) copy-start(bf16[8,64,64]{2,1,0:T(8,128)(2,1)} %maps.1) | copy-start | bytes 196612
  31.6 22.1 %copy-start.4 = (f32[64,64]{1,0:T(8,128)S(1)}, f32[64,64]{1,0:T(8,128)}, u32[]{:S(2)}) copy-start(f32[64,64]{1,0:T(8,128)} %parent.1) | copy-start | bytes 49156
